TPU v7x, 256 devices: a whole 4x4x8 slice. The times are simulated.
256 devices in a mesh: feat: 8 (over y, core), node: 32 (over x, z).
Axes of the slice: x: 4, y: 4, z: 8, core: 2. Of those that a mesh axis runs over, the one named last changes fastest.
Arguments:
- node_feats: float32 [256, 131072], P('feat', 'node'), may hold values from -6 to 6
- tiles: float32 [1024, 4, 128, 128], P('node'), may hold values from -0.5 to 0.5
- send_col: int32 [1024, 4], P('node'), may hold values from 0 to 31
- recv_row: int32 [1024, 4], P('node'), may hold values from -1 to 31, as said below
- degree: int32 [131072], P('node'), may hold values from 1 to 8
- w_self: float32 [256, 256], replicated, may hold values from -0.375 to 0.375
- w_neigh: float32 [256, 256], replicated, may hold values from -0.375 to 0.375
- bias: float32 [256], replicated, may hold values from -3 to 3
- cotangent: float32 [131072, 256], P(('node', 'feat')), may hold values from -24 to 24
Outputs:
- activated: float32 [131072, 256], P(('node', 'feat'))
- grad_feats: float32 [256, 131072], P('feat', 'node')
- grad_self: float32 [256, 256], replicated
- grad_neigh: float32 [256, 256], replicated
- grad_bias: float32 [256], replicated
Inputs may be any that keep to these rules, and one draw needn't show every extreme that they name: `recv_row`: at most 4 live slots from one sender to one owner; every sender fills all 4 slots to itself, and one owner receives 4 live slots from every sender; -1 marks an empty slot.
All inputs are finite; a program needn't handle non-finite values.
Results may differ from a plain program's by a relative error of at most 0.0003.
Values sent between devices are 32-bit elements; how exact they have to be, the bound alone decides.
A program may use at most 64 MiB of HBM per device.

v0:
```python
import jax
import jax.numpy as jnp
from jax import lax
from jax.sharding import PartitionSpec as P

TB = 128


def shards(node_feats, tiles, send_col, recv_row, degree, w_self, w_neigh, bias, cotangent):
    slices, owned = node_feats.shape
    blocks = owned // TB
    block_ids = jnp.arange(blocks, dtype=jnp.int32)
    scale = degree.astype(jnp.float32)[None, :]
    col_onehot = (send_col[..., None] == block_ids).astype(jnp.float32)
    row_onehot = (recv_row[..., None] == block_ids).astype(jnp.float32)
    feat_blocks = node_feats.reshape(slices, blocks, TB)
    picked = jnp.einsum("dcb,fbj->dcfj", col_onehot, feat_blocks, precision=lax.Precision.HIGHEST)
    partial_value = jnp.einsum("dcfj,dcij->dcfi", picked, tiles, precision=lax.Precision.HIGHEST)
    arrived = lax.all_to_all(partial_value, "node", split_axis=0, concat_axis=0, tiled=True)
    summed = jnp.einsum("scfi,scb->fbi", arrived, row_onehot, precision=lax.Precision.HIGHEST)
    neighbour = summed.reshape(slices, owned) / scale
    offset = lax.axis_index("feat") * slices
    self_rows = lax.dynamic_slice_in_dim(w_self, offset, slices, 0)
    neigh_rows = lax.dynamic_slice_in_dim(w_neigh, offset, slices, 0)
    first = lax.dot_general(
        node_feats, self_rows, (((0,), (0,)), ((), ())), precision=lax.Precision.HIGHEST
    )
    second = lax.dot_general(
        neighbour, neigh_rows, (((0,), (0,)), ((), ())), precision=lax.Precision.HIGHEST
    )
    pre = lax.psum_scatter(first + second, "feat", scatter_dimension=0, tiled=True) + bias
    sigma = jax.nn.sigmoid(pre)
    activated = pre * sigma
    gpre = cotangent * sigma * (1.0 + pre * (1.0 - sigma))
    piece = lax.all_gather(gpre, "feat", axis=0, tiled=True)
    self_back = lax.dot_general(
        self_rows, piece, (((1,), (1,)), ((), ())), precision=lax.Precision.HIGHEST
    )
    neigh_back = lax.dot_general(
        neigh_rows, piece, (((1,), (1,)), ((), ())), precision=lax.Precision.HIGHEST
    )
    gathered = piece.T
    slice_self = lax.dot_general(
        node_feats, gathered, (((1,), (1,)), ((), ())), precision=lax.Precision.HIGHEST
    )
    slice_neigh = lax.dot_general(
        neighbour, gathered, (((1,), (1,)), ((), ())), precision=lax.Precision.HIGHEST
    )
    grad_bias_part = jnp.sum(gathered, axis=1)
    slice_self, slice_neigh, grad_bias = lax.psum((slice_self, slice_neigh, grad_bias_part), "node")
    grad_self, grad_neigh = (
        lax.all_gather(slice_self, "feat", axis=0, tiled=True),
        lax.all_gather(slice_neigh, "feat", axis=0, tiled=True),
    )
    gneigh = (neigh_back / scale).reshape(slices, blocks, TB)
    outgoing = jnp.einsum("scb,fbi->scfi", row_onehot, gneigh, precision=lax.Precision.HIGHEST)
    returned = lax.all_to_all(outgoing, "node", split_axis=0, concat_axis=0, tiled=True)
    spread = jnp.einsum("dcfi,dcij->dcfj", returned, tiles, precision=lax.Precision.HIGHEST)
    placed = jnp.einsum("dcfj,dcb->fbj", spread, col_onehot, precision=lax.Precision.HIGHEST)
    grad_feats = self_back + placed.reshape(slices, owned)
    return (activated, grad_feats, grad_self, grad_neigh, grad_bias)


def solution(mesh):
    return jax.shard_map(
        shards,
        mesh=mesh,
        in_specs=(
            P("feat", "node"),
            P("node", None, None, None),
            P("node", None),
            P("node", None),
            P("node"),
            P(),
            P(),
            P(),
            P(("node", "feat"), None),
        ),
        out_specs=(P(("node", "feat"), None), P("feat", "node"), P(), P(), P()),
        check_vma=False,
    )
```

profile of v0, /device:TPU:1, one launch (start us, length us, event | category | flops | bytes accessed | tf_op | source)
XLA Modules:
  0.0 401.0 jit_solution(9033318631979947825)
XLA Ops:
  7.2 1.2 copy.30
  8.4 1.7 fusion.17
  10.1 16.1 %fusion.2 = f32[32,4,32,128]{3,2,1,0:T(8,128)S(1)} fusion(f32[32,4,128,128]{3,2,1,0:T(8,128)} %param.10, f32[32,4,32,128]{3,0,2,1:T(8,128)S(1)} %fusion.17), kind=kOutput, calls=%fused_computation.6 | convolution fusion | flops 805306368 | bytes 12582912 | tf_op jit(solution)/shard_map/dcfj,dcij->dcfi/dot_general | solution.py:18
  26.1 3.1 copy.23
  29.3 12.0 %all-to-all-start = ((f32[32,4,32,128]{3,1,2,0:T(4,128)}), f32[32,4,32,128]{3,1,2,0:T(4,128)S(1)}, u32[]{:S(2)}, u32[]{:S(2)}) async-start(f32[32,4,32,128]{3,1,2,0:T(4,128)} %copy.23), calls=%async_computation | async-start | bytes 4194304 | tf_op jit(solution)/shard_map/all_to_all | solution.py:19
  41.6 5.8 %convolution_bitcast_fusion = f32[4096,256]{0,1:T(8,128)} fusion(f32[32,4096]{1,0:T(8,128)S(1)} %copy-done.3, f32[256,256]{1,0:T(8,128)} %param.14, s32[]{:T(128)S(6)} %select_n.4), kind=kOutput, calls=%fused_computation.1 | convolution fusion | flops 402653184 | bytes 4751364 | tf_op jit(solution)/shard_map/dot_general | solution.py:25
  47.4 42.8 %all-to-all-done = f32[32,4,32,128]{3,1,2,0:T(4,128)S(1)} async-done(((f32[32,4,32,128]{3,1,2,0:T(4,128)}), f32[32,4,32,128]{3,1,2,0:T(4,128)S(1)}, u32[]{:S(2)}, u32[]{:S(2)}) %all-to-all-start) | async-done | bytes 2097184 | tf_op jit(solution)/shard_map/all_to_all | solution.py:19
  90.2 2.1 fusion.4
  92.3 6.8 %convolution_add_fusion = f32[4096,256]{0,1:T(8,128)} fusion(f32[4096,256]{0,1:T(8,128)} %convolution_bitcast_fusion, f32[4,8,32,128]{3,2,1,0:T(8,128)S(1)} %bitcast.55, f32[4096]{0:T(1024)S(1)} %convert_element_type.2, f32[256,256]{1,0:T(8,128)S(1)} %copy-done, s32[]{:T(128)S(6)} %select_n.4), kind=kOutput, calls=%fused_computation | convolution fusion | flops 403832832 | bytes 8962052 | tf_op jit(solution)/shard_map/dot_general | solution.py:28
  100.4 35.6 %reduce-scatter.2.cloned.1.call-done = f32[512,256]{0,1:T(8,128)} async-done(((f32[4096,256]{0,1:T(8,128)}), f32[512,256]{0,1:T(8,128)}) %reduce-scatter.2.cloned.1.call-update) | async-done | bytes 524304 | tf_op jit(solution)/shard_map/reduce_scatter | solution.py:31
  136.0 2.3 add_multiply_fusion
  138.3 37.3 %all-gather.2.cloned.1.call-done = f32[4096,256]{0,1:T(8,128)} async-done(((f32[512,256]{0,1:T(8,128)}), f32[4096,256]{0,1:T(8,128)}) %all-gather.2.cloned.1.call-update) | async-done | bytes 4194320 | tf_op jit(solution)/shard_map/all_gather | solution.py:35
  175.6 4.7 %fusion.6 = f32[4,8,32,128]{3,1,2,0:T(8,128)S(1)} fusion(f32[4096,256]{0,1:T(8,128)} %all-gather.2.cloned.1.call-done, f32[4096]{0:T(1024)S(1)} %convert_element_type.2, f32[256,256]{1,0:T(8,128)S(1)} %copy-done, s32[]{:T(128)S(6)} %select_n.4), kind=kOutput, calls=%fused_computation.10 | convolution fusion | flops 402784256 | bytes 4767748 | tf_op jit(solution)/shard_map/dot_general | solution.py:39
  181.4 2.6 copy.27
  184.0 9.5 %all-to-all-start.1 = ((f32[32,4,32,128]{3,2,1,0:T(8,128)}), f32[32,4,32,128]{3,2,1,0:T(8,128)S(1)}, u32[]{:S(2)}, u32[]{:S(2)}) async-start(f32[32,4,32,128]{3,2,1,0:T(8,128)} %copy.27), calls=%async_computation.2 | async-start | bytes 4194304 | tf_op jit(solution)/shard_map/all_to_all | solution.py:57
  193.8 3.0 reduce_sum.9
  196.8 6.6 %convolution_bitcast_fusion.1 = f32[32,256]{1,0:T(8,128)} fusion(f32[4096,256]{0,1:T(8,128)} %all-gather.2.cloned.1.call-done, f32[32,4096]{1,0:T(8,128)S(1)} %copy-done.3), kind=kOutput, calls=%fused_computation.11 | convolution fusion | flops 402653184 | bytes 4751360 | tf_op jit(solution)/shard_map/dot_general | solution.py:43
  203.5 4.4 %fusion.8 = f32[32,256]{1,0:T(8,128)} fusion(f32[4096,256]{0,1:T(8,128)S(1)} %copy-done.1, f32[4,8,32,128]{3,2,1,0:T(8,128)S(1)} %bitcast.56, f32[4096]{0:T(1024)S(1)} %convert_element_type.2), kind=kOutput, calls=%fused_computation.16 | convolution fusion | flops 402784256 | bytes 4767744 | tf_op jit(solution)/shard_map/dot_general | solution.py:46
  208.9 136.1 %all-reduce.3.cloned.1.call-done = (f32[32,256]{1,0:T(8,128)}, f32[32,256]{1,0:T(8,128)}, f32[256]{0:T(256)}) async-done(((f32[32,256]{1,0:T(8,128)}, f32[32,256]{1,0:T(8,128)}, f32[256]{0:T(256)}), (f32[32,256]{1,0:T(8,128)}, f32[32,256]{1,0:T(8,128)}, f32[256]{0:T(256)})) %all-reduce.3.cloned.1.call-update) | async-done | bytes 66576 | tf_op jit(solution)/shard_map/psum | solution.py:50
  345.0 18.2 %all_gather.10 = f32[256,256]{1,0:T(8,128)S(1)} all-gather(f32[32,256]{1,0:T(8,128)} %get-tuple-element.15), channel_id=1, replica_groups=mesh['feat'=8,'node'=32] {'feat'}, dimensions={0}, use_global_device_ids=true | all-gather | bytes 294912 | tf_op jit(solution)/shard_map/all_gather | solution.py:52
  363.2 13.3 %all_gather.11 = f32[256,256]{1,0:T(8,128)S(1)} all-gather(f32[32,256]{1,0:T(8,128)} %get-tuple-element.16), channel_id=1, replica_groups=mesh['feat'=8,'node'=32] {'feat'}, dimensions={0}, use_global_device_ids=true | all-gather | bytes 294912 | tf_op jit(solution)/shard_map/all_gather | solution.py:53
  376.5 9.7 %fusion.31 = f32[32,4,32,128]{3,2,1,0:T(8,128)S(1)} fusion(f32[32,4,32,128]{3,2,1,0:T(8,128)S(1)} %all-to-all-done.1, f32[32,4,128,128]{3,2,1,0:T(8,128)} %param.10), kind=kOutput, calls=%fused_computation.37 | convolution fusion | flops 805306368 | bytes 12582912 | tf_op jit(solution)/shard_map/dcfi,dcij->dcfj/dot_general | solution.py:58
  386.2 2.1 fusion
  388.3 4.2 %convolution_add_fusion.1 = f32[32,4096]{1,0:T(8,128)} fusion(f32[4096,256]{0,1:T(8,128)S(1)} %copy-done.2, f32[4,8,32,128]{3,2,1,0:T(8,128)S(1)} %bitcast.59, f32[256,256]{1,0:T(8,128)} %param.14, s32[]{:T(128)S(6)} %select_n.4), kind=kOutput, calls=%fused_computation.3 | convolution fusion | flops 402784256 | bytes 5275652 | tf_op jit(solution)/shard_map/dot_general | solution.py:36
  (37 shorter events, 5.9 us)
Async XLA Ops:
  7.2 85.1 %copy-start = (f32[256,256]{1,0:T(8,128)S(1)}, f32[256,256]{1,0:T(8,128)}, u32[]{:S(2)}) copy-start(f32[256,256]{1,0:T(8,128)} %param.15) | copy-start | bytes 786436
  29.3 12.2 %copy-start.6 = (s32[4096]{0:T(1024)S(1)}, s32[4096]{0:T(1024)}, u32[]{:S(2)}) copy-start(s32[4096]{0:T(1024)} %param.13) | copy-start | bytes 49156
  29.3 12.3 %copy-start.3 = (f32[32,4096]{1,0:T(8,128)S(1)}, f32[32,4096]{1,0:T(8,128)}, u32[]{:S(2)}) copy-start(f32[32,4096]{1,0:T(8,128)} %param.9) | copy-start | bytes 1572868
  29.3 60.9 %all-to-all-start = ((f32[32,4,32,128]{3,1,2,0:T(4,128)}), f32[32,4,32,128]{3,1,2,0:T(4,128)S(1)}, u32[]{:S(2)}, u32[]{:S(2)}) async-start(f32[32,4,32,128]{3,1,2,0:T(4,128)} %copy.23), calls=%async_computation | async-start | bytes 4194304 | tf_op jit(solution)/shard_map/all_to_all | solution.py:19
  41.3 94.7 %reduce-scatter.2.cloned.1.call-start = ((), (), s32[]{:S(2)}) async-start(), calls=%async_computation.3 | async-start | bytes 4718592 | tf_op jit(solution)/shard_map/reduce_scatter | solution.py:31
  41.6 48.6 %copy-start.7 = (s32[32,4]{0,1:T(4,128)S(1)}, s32[32,4]{0,1:T(4,128)}, u32[]{:S(2)}) copy-start(s32[32,4]{0,1:T(4,128)} %param.12) | copy-start | bytes 1540
  99.1 1.0 copy-start.5
  99.1 36.8 %copy-start.9 = (f32[256]{0:T(256)S(1)}, f32[256]{0:T(256)}, u32[]{:S(2)}) copy-start(f32[256]{0:T(256)} %param.16) | copy-start | bytes 3076
  99.2 76.4 %all-gather.2.cloned.1.call-start = ((), (), s32[]{:S(2)}) async-start(), calls=%async_computation.4 | async-start | bytes 4718592 | tf_op jit(solution)/shard_map/all_gather | solution.py:35
  184.0 192.5 %all-to-all-start.1 = ((f32[32,4,32,128]{3,2,1,0:T(8,128)}), f32[32,4,32,128]{3,2,1,0:T(8,128)S(1)}, u32[]{:S(2)}, u32[]{:S(2)}) async-start(f32[32,4,32,128]{3,2,1,0:T(8,128)} %copy.27), calls=%async_computation.2 | async-start | bytes 4194304 | tf_op jit(solution)/shard_map/all_to_all | solution.py:57
  193.5 151.5 %all-reduce.3.cloned.1.call-start = ((), (), s32[]{:S(2)}) async-start(), calls=%async_computation.5 | async-start | bytes 133120 | tf_op jit(solution)/shard_map/psum | solution.py:50
  196.8 6.6 %copy-start.1 = (f32[4096,256]{0,1:T(8,128)S(1)}, f32[4096,256]{0,1:T(8,128)}, u32[]{:S(2)}) copy-start(f32[4096,256]{0,1:T(8,128)} %all-gather.2.cloned.1.call-done) | copy-start | bytes 12582916
  203.5 4.4 %copy-start.4 = (f32[512,256]{0,1:T(8,128)S(1)}, f32[512,256]{0,1:T(8,128)}, u32[]{:S(2)}) copy-start(f32[512,256]{0,1:T(8,128)} %get-tuple-element.19) | copy-start | bytes 1572868
  376.5 9.7 %copy-start.8 = (s32[32,4]{0,1:T(4,128)S(1)}, s32[32,4]{0,1:T(4,128)}, u32[]{:S(2)}) copy-start(s32[32,4]{0,1:T(4,128)} %param.11) | copy-start | bytes 1540
  376.5 11.8 %copy-start.2 = (f32[4096,256]{0,1:T(8,128)S(1)}, f32[4096,256]{0,1:T(8,128)}, u32[]{:S(2)}) copy-start(f32[4096,256]{0,1:T(8,128)} %all-gather.2.cloned.1.call-done) | copy-start | bytes 12582916
  388.3 5.6 %copy-start.10 = (f32[256]{0:T(256)S(1)}, f32[256]{0:T(256)}, u32[]{:S(2)}) copy-start(f32[256]{0:T(256)} %get-tuple-element.29) | copy-start | bytes 3076
Sparse Core Ops, SparseCore 0:
  99.3 36.6 reduce-scatter.1
  138.4 37.1 all-gather.1
  208.0 136.9 all-reduce.2
where the time goes:
time: 402 us; the launch traced here: 401 us
  waiting for transfers between devices  252 us (63%)
  matrix products  65.2 us (16%)
  blocking collectives  31.5 us (8%)
  starting transfers between devices  22.1 us (5%)
  between operations  13.9 us (3%)
  local copies, waits for them, and re-layouts  11.2 us (3%)
  other arithmetic  5.33 us (1%)
    psum x1, waiting for transfers between devices, shards(): lax.psum((slice_self, slice_neigh, grad_bias_part), 'node')  136 us
    all_to_all x1, waiting for transfers between devices, shards(): lax.all_to_all(partial_value, 'node', split_axis=0, concat_axis=0, tiled=...  42.8 us
    all_gather x1, waiting for transfers between devices, shards(): piece = lax.all_gather(gpre, 'feat', axis=0, tiled=True)  37.3 us
    reduce_scatter x1, waiting for transfers between devices, shards(): lax.psum_scatter(first + second, 'feat', scatter_dimension=0, tiled=True)  35.6 us
    all_gather x1, blocking collectives, shards(): lax.all_gather(slice_self, 'feat', axis=0, tiled=True)  18.2 us
    dot_general x1, matrix products, shards(): jnp.einsum('dcfj,dcij->dcfi', picked, tiles, precision=lax.Precision.HIGH...  16.1 us
    all_gather x1, blocking collectives, shards(): lax.all_gather(slice_neigh, 'feat', axis=0, tiled=True)  13.3 us
    all_to_all x1, starting transfers between devices, shards(): lax.all_to_all(partial_value, 'node', split_axis=0, concat_axis=0, tiled=...  12 us
  transfers between devices with their start and end apart: 5, of which 4 were waited for; matrix products, arithmetic and copies ran while one was open for 5% of the time, Pallas kernels for 0%

commit v1 on v0

v1 whole, which is shorter than its diff:
```python
import functools

import jax
import jax.numpy as jnp
from jax import lax
from jax.experimental import pallas as pl
from jax.experimental.pallas import tpu as pltpu
from jax.sharding import PartitionSpec as P

TB = 128
CAP = 4
NX = 4
NCH = 2
BF = jnp.bfloat16
F32 = jnp.float32
NN_DIMS = (((1,), (0,)), ((), ()))
NT_DIMS = (((1,), (1,)), ((), ()))


def split(x):
    hi = x.astype(BF)
    return hi, (x - hi.astype(F32)).astype(BF)


def dot(a, b, dims):
    return lax.dot_general(a, b, dims, preferred_element_type=F32)


def dot3(a, b, dims):
    return dot(a[0], b[0], dims) + dot(a[0], b[1], dims) + dot(a[1], b[0], dims)


def kernel(
    nn, nf, nx,
    feats, tiles, scol, rrow, deg, wself, wneigh, bias, cot,
    act_o, gf_o, gs_o, gn_o, gb_o,
    tv, fs, sb, rb, acc, xall, nsd, nall, wsh, wsl, wsth, wstl, wnh, wnl, wnth, wntl,
    cott, pret, gh, gl, act_v, gsd, grc, ssd, srv, bsd, brv, acc2, gf_v,
    r1s, r1r, r2s, r2r, r3s, r3r, r4s, r4r, outw, gb_v,
    tsem, xss, xrs, fss, frs, nss, nrs, gss, grs, sss, srs, bss, brs,
    r1ss, r1rs, r2ss, r2rs, r3ss, r3rs, r4ss, r4rs, r5ss, r5rs, osem,
):
    nz = nn // nx
    F = feats.shape[0]
    nblk = feats.shape[1] // TB
    Q = nblk // nf
    H = wself.shape[0]
    FC = F // NCH
    RZ = 2 * F // nz
    mf, mn = lax.axis_index("feat"), lax.axis_index("node")
    mx, mz = mn // nz, mn % nz

    def offset(j):
        dx = (j + 1) % nx
        t = j // nx
        dz = (nz // 2 + (1 - 2 * (t % 2)) * ((t + 1) // 2) + nz) % nz
        return dx, dz

    def target(j):
        dx, dz = offset(j)
        return ((mx + dx) % nx) * nz + (mz + dz) % nz

    def source(j):
        dx, dz = offset(j)
        return ((mx - dx + nx) % nx) * nz + (mz - dz + nz) % nz

    def remote(src, dst, ss, rs, **where):
        return pltpu.make_async_remote_copy(
            src_ref=src, dst_ref=dst, send_sem=ss, recv_sem=rs,
            device_id=where, device_id_type=pl.DeviceIdType.MESH,
        )

    barrier = pltpu.get_barrier_semaphore()

    @pl.loop(0, nn)
    def _(j):
        d = target(j)
        pltpu.make_async_copy(tiles.at[d], tv.at[d], tsem.at[d]).start()

    @pl.loop(1, nn)
    def _(k):
        pl.semaphore_signal(barrier, inc=1, device_id={"node": (mn + k) % nn},
                            device_id_type=pl.DeviceIdType.MESH)

    @pl.loop(1, nf)
    def _(k):
        pl.semaphore_signal(barrier, inc=1, device_id={"feat": (mf + k) % nf},
                            device_id_type=pl.DeviceIdType.MESH)

    for b in range(nblk):
        hi, lo = split(feats[:, b * TB:(b + 1) * TB])
        fs[b, :F] = hi
        fs[b, F:] = lo
    acc[...] = jnp.zeros_like(acc)
    acc2[...] = jnp.zeros_like(acc2)
    pl.semaphore_wait(barrier, nn - 1 + nf - 1)

    def x_copy(to):
        cols = pl.ds(pl.multiple_of(to * (Q * TB), Q * TB), Q * TB)
        rows = pl.ds(pl.multiple_of(mf * F, F), F)
        return remote(feats.at[:, cols], xall.at[rows, :], xss.at[to], xrs.at[mf], feat=to)

    @pl.loop(1, nf)
    def _(k):
        x_copy((mf + k) % nf).start()

    own_rows = pl.ds(pl.multiple_of(mf * F, F), F)
    xall[own_rows, :] = feats[:, pl.ds(pl.multiple_of(mf * (Q * TB), Q * TB), Q * TB)]

    def f_copy(h, d):
        return remote(sb.at[h, d], rb.at[h, mn], fss.at[h, d], frs.at[h, mn], node=d)

    def tile_forward(d):
        pltpu.make_async_copy(tiles.at[d], tv.at[d], tsem.at[d]).wait()
        for c in range(CAP):
            lhs = fs[scol[d, c]]
            th, tl = split(tv[d, c])
            o = dot(lhs, th, NT_DIMS)
            res = o[:F] + o[F:] + dot(lhs[:F], tl, NT_DIMS)
            for h in range(NCH):
                sb[h, d, c] = res[h * FC:(h + 1) * FC]

    @pl.loop(0, nn - 1)
    def _(j):
        d = target(j)
        tile_forward(d)
        f_copy(0, d).start()

    @pl.loop(0, (NCH - 1) * (nn - 1))
    def _(k):
        f_copy(1 + k // (nn - 1), target(k % (nn - 1))).start()

    tile_forward(mn)

    ws = wself[...]
    wsh[...], wsl[...] = split(ws)
    wsth[...], wstl[...] = split(ws.T)
    for h in range(NCH):
        rows = jnp.concatenate(
            [wneigh[f * F + h * FC:f * F + (h + 1) * FC, :] for f in range(nf)], axis=0)
        wnh[h], wnl[h] = split(rows)
        wnth[h], wntl[h] = split(rows.T)
    for q in range(Q):
        cott[:, q * TB:(q + 1) * TB] = cot[q * TB:(q + 1) * TB, :].T
    bias_t = jnp.broadcast_to(bias[...], (TB, H)).T

    @pl.loop(1, nf)
    def _(k):
        frm = (mf + nf - k) % nf
        rows = pl.ds(pl.multiple_of(frm * F, F), F)
        remote(xall.at[rows, :], xall.at[rows, :], xss.at[frm], xrs.at[frm], feat=frm).wait_recv()

    for q in range(Q):
        cols = slice(q * TB, (q + 1) * TB)
        pret[:, cols] = bias_t + dot3((wsth[...], wstl[...]), split(xall[:, cols]), NN_DIMS)

    def place(h, s, ref):
        vals = [ref[h, s, c] for c in range(CAP)]
        dest = [rrow[s, c] for c in range(CAP)]

        @pl.loop(0, nblk // 8)
        def _(g):
            for i in range(8):
                b = g * 8 + i
                a = acc[h, b]
                for c in range(CAP):
                    a = a + vals[c] * jnp.where(dest[c] == b, 1.0, 0.0)
                acc[h, b] = a

    def n_copy(h, to):
        return remote(nsd.at[h, to], nall.at[h, mf], nss.at[h, to], nrs.at[h, mf], feat=to)

    for h in range(NCH):
        place(h, mn, sb)

        @pl.loop(0, nn - 1)
        def _(j):
            s = source(j)
            remote(sb.at[h, s], rb.at[h, s], fss.at[h, s], frs.at[h, s], node=s).wait_recv()
            place(h, s, rb)

        @pl.loop(0, nf)
        def _(f):
            for q in range(Q):
                nsd[h, f, :, q * TB:(q + 1) * TB] = acc[h, f * Q + q]

        @pl.loop(1, nf)
        def _(k):
            n_copy(h, (mf + k) % nf).start()

        nall[h, mf] = nsd[h, mf]

    inv = [1.0 / deg[mf * Q + q].astype(F32) for q in range(Q)]
    for h in range(NCH):
        @pl.loop(1, nf)
        def _(k):
            frm = (mf + nf - k) % nf
            remote(nsd.at[h, frm], nall.at[h, frm], nss.at[h, frm], nrs.at[h, frm], feat=frm).wait_recv()

        for q in range(Q):
            cols = slice(q * TB, (q + 1) * TB)
            nb = nall[h, :, :, cols].reshape(nf * FC, TB) * inv[q]
            nall[h, :, :, cols] = nb.reshape(nf, FC, TB)
            pre = pret[:, cols] + dot3((wnth[h], wntl[h]), split(nb), NN_DIMS)
            pret[:, cols] = pre
            if h == NCH - 1:
                sig = 1.0 / (1.0 + jnp.exp(-pre))
                act_v[cols, :] = (pre * sig).T
                g = cott[:, cols] * (sig * (1.0 + pre * (1.0 - sig)))
                gh[:, cols], gl[:, cols] = split(g)
    act_copy = pltpu.make_async_copy(act_v, act_o, osem.at[0])
    act_copy.start()

    def g_copy(h, to):
        blocks = pl.ds(pl.multiple_of(mf * Q, Q), Q)
        return remote(gsd.at[h, to], grc[h].at[blocks], gss.at[h, to], grs.at[h, mf], feat=to)

    for h in range(NCH):
        for q in range(Q):
            cols = slice(q * TB, (q + 1) * TB)
            back = dot3((wnh[h], wnl[h]), (gh[:, cols], gl[:, cols]), NN_DIMS) * inv[q]
            for f in range(nf):
                gsd[h, f, q] = back[f * FC:(f + 1) * FC]

        @pl.loop(1, nf)
        def _(k):
            g_copy(h, (mf + k) % nf).start()

        for q in range(Q):
            grc[h][mf * Q + q] = gsd[h, mf, q]

    def r1_copy(to):
        return remote(r1s.at[to], r1r.at[mf], r1ss.at[to], r1rs.at[mf], feat=to)

    part_self = dot3(split(xall[...]), (gh[...], gl[...]), NT_DIMS)
    for f in range(nf):
        r1s[f, :F] = part_self[f * F:(f + 1) * F]
    for h in range(NCH):
        part = dot3(split(nall[h].reshape(nf * FC, Q * TB)), (gh[...], gl[...]), NT_DIMS)
        for f in range(nf):
            r1s[f, F + h * FC:F + (h + 1) * FC] = part[f * FC:(f + 1) * FC]
    ones = jnp.ones((16, Q * TB), BF)
    part_bias = (dot(ones, gh[...], NT_DIMS) + dot(ones, gl[...], NT_DIMS))[:8]
    for f in range(nf):
        r1s[f, 2 * F:] = part_bias

    def b_copy(h, d):
        return remote(bsd.at[h, d], brv.at[h, mn], bss.at[h, d], brs.at[h, mn], node=d)

    def pick(h, s, ref, at):
        for c in range(CAP):
            r = rrow[s, c]
            ref[h, at, c] = grc[h][jnp.maximum(r, 0)] * jnp.where(r >= 0, 1.0, 0.0)

    for h in range(NCH):
        @pl.loop(1, nf)
        def _(k):
            frm = (mf + nf - k) % nf
            blocks = pl.ds(pl.multiple_of(frm * Q, Q), Q)
            remote(gsd.at[h, frm], grc[h].at[blocks], gss.at[h, frm], grs.at[h, frm], feat=frm).wait_recv()

        @pl.loop(0, nn - 1)
        def _(j):
            d = target(j)
            pick(h, d, bsd, d)
            b_copy(h, d).start()

        pick(h, mn, brv, mn)

    @pl.loop(1, nf)
    def _(k):
        r1_copy((mf + k) % nf).start()

    r1r[mf] = r1s[mf]

    def s_copy(to):
        blocks = pl.ds(pl.multiple_of(mf * Q, Q), Q)
        return remote(ssd.at[to], srv.at[blocks], sss.at[to], srs.at[mf], feat=to)

    for q in range(Q):
        cols = slice(q * TB, (q + 1) * TB)
        back = dot3((wsh[...], wsl[...]), (gh[:, cols], gl[:, cols]), NN_DIMS)
        for f in range(nf):
            ssd[f, q] = back[f * F:(f + 1) * F]

    @pl.loop(1, nf)
    def _(k):
        s_copy((mf + k) % nf).start()

    for q in range(Q):
        srv[mf * Q + q] = ssd[mf, q]

    def tile_backward(d):
        outs = []
        for c in range(CAP):
            a = jnp.concatenate([brv[h, d, c] for h in range(NCH)], axis=0)
            ah, al = split(a)
            th, tl = split(tv[d, c])
            o = dot(jnp.concatenate([ah, al], axis=0), th, NN_DIMS)
            outs.append(o[:F] + o[F:] + dot(ah, tl, NN_DIMS))
        dest = [scol[d, c] for c in range(CAP)]

        @pl.loop(0, nblk // 8)
        def _(g):
            for i in range(8):
                b = g * 8 + i
                a = acc2[b]
                for c in range(CAP):
                    a = a + outs[c] * jnp.where(dest[c] == b, 1.0, 0.0)
                acc2[b] = a

    def backward_steps(start, stop):
        @pl.loop(start, stop)
        def _(j):
            d = source(j)
            for h in range(NCH):
                remote(bsd.at[h, d], brv.at[h, d], bss.at[h, d], brs.at[h, d], node=d).wait_recv()
            tile_backward(d)

    tile_backward(mn)

    @pl.loop(1, nf)
    def _(k):
        frm = (mf + nf - k) % nf
        remote(r1s.at[frm], r1r.at[frm], r1ss.at[frm], r1rs.at[frm], feat=frm).wait_recv()

    for z in range(nz):
        rows = slice(z * RZ, (z + 1) * RZ)
        r2s[z, :RZ] = sum((r1r[f, rows] for f in range(1, nf)), r1r[0, rows])
    bias_sum = sum((r1r[f, 2 * F:] for f in range(1, nf)), r1r[0, 2 * F:])
    for z in range(nz):
        r2s[z, RZ:] = bias_sum

    def r2_copy(z):
        return remote(r2s.at[z], r2r.at[mz], r2ss.at[z], r2rs.at[mz], node=mx * nz + z)

    @pl.loop(1, nz)
    def _(k):
        r2_copy((mz + k) % nz).start()

    r2r[mz] = r2s[mz]
    step = (nn - 1) // 4
    backward_steps(0, step)

    @pl.loop(1, nz)
    def _(k):
        z = (mz + nz - k) % nz
        remote(r2s.at[z], r2r.at[z], r2ss.at[z], r2rs.at[z], node=mx * nz + z).wait_recv()

    r3s[...] = sum((r2r[z] for z in range(1, nz)), r2r[0])

    def r3_copy(x):
        return remote(r3s, r3r.at[mx], r3ss.at[x], r3rs.at[mx], node=x * nz + mz)

    @pl.loop(1, nx)
    def _(k):
        r3_copy((mx + k) % nx).start()

    r3r[mx] = r3s[...]
    backward_steps(step, 2 * step)

    @pl.loop(1, nx)
    def _(k):
        x = (mx + nx - k) % nx
        remote(r3s, r3r.at[x], r3ss.at[x], r3rs.at[x], node=x * nz + mz).wait_recv()

    total = sum((r3r[x] for x in range(1, nx)), r3r[0])
    r4s[...] = total[:RZ]
    gb_v[...] = total[RZ:RZ + 1]

    def r4_copy(z):
        return remote(r4s, r4r.at[mz], r4ss.at[z], r4rs.at[mz], node=mx * nz + z)

    @pl.loop(1, nz)
    def _(k):
        r4_copy((mz + k) % nz).start()

    r4r[mz] = r4s[...]
    backward_steps(2 * step, 3 * step)

    @pl.loop(1, nz)
    def _(k):
        z = (mz + nz - k) % nz
        remote(r4s, r4r.at[z], r4ss.at[z], r4rs.at[z], node=mx * nz + z).wait_recv()

    def r5_copy(i, to):
        part = r4r.at[pl.ds(i * (nz // 2), nz // 2)]
        rows = pl.ds(pl.multiple_of(mf * nz // 2, nz // 2), nz // 2)
        return remote(part, outw.at[i, rows], r5ss.at[i, to], r5rs.at[i, mf], feat=to)

    for i in range(2):
        @pl.loop(1, nf)
        def _(k):
            r5_copy(i, (mf + k) % nf).start()

        for z in range(nz // 2):
            outw[i, mf * (nz // 2) + z] = r4r[i * (nz // 2) + z]
    backward_steps(3 * step, nn - 1)

    @pl.loop(1, nf)
    def _(k):
        frm = (mf + nf - k) % nf
        blocks = pl.ds(pl.multiple_of(frm * Q, Q), Q)
        remote(ssd.at[frm], srv.at[blocks], sss.at[frm], srs.at[frm], feat=frm).wait_recv()

    for b in range(nblk):
        gf_v[:, b * TB:(b + 1) * TB] = srv[b] + acc2[b]
    gf_copy = pltpu.make_async_copy(gf_v, gf_o, osem.at[1])
    gf_copy.start()
    for i in range(2):
        @pl.loop(1, nf)
        def _(k):
            frm = (mf + nf - k) % nf
            part = r4r.at[pl.ds(i * (nz // 2), nz // 2)]
            rows = pl.ds(pl.multiple_of(frm * nz // 2, nz // 2), nz // 2)
            remote(part, outw.at[i, rows], r5ss.at[i, frm], r5rs.at[i, frm], feat=frm).wait_recv()
    tail = [
        pltpu.make_async_copy(outw.at[0], gs_o, osem.at[2]),
        pltpu.make_async_copy(outw.at[1], gn_o, osem.at[3]),
        pltpu.make_async_copy(gb_v, gb_o, osem.at[4]),
    ]
    for copy in tail:
        copy.start()

    @pl.loop(1, nf)
    def _(k):
        to = (mf + k) % nf
        x_copy(to).wait_send()
        r1_copy(to).wait_send()
        s_copy(to).wait_send()
        for h in range(NCH):
            n_copy(h, to).wait_send()
            g_copy(h, to).wait_send()
        for i in range(2):
            r5_copy(i, to).wait_send()

    @pl.loop(1, nz)
    def _(k):
        z = (mz + k) % nz
        r2_copy(z).wait_send()
        r4_copy(z).wait_send()

    @pl.loop(1, nx)
    def _(k):
        r3_copy((mx + k) % nx).wait_send()

    @pl.loop(0, nn - 1)
    def _(j):
        d = target(j)
        for h in range(NCH):
            f_copy(h, d).wait_send()
            b_copy(h, d).wait_send()

    act_copy.wait()
    gf_copy.wait()
    for copy in tail:
        copy.wait()


def shards(nn, nf, nx, node_feats, tiles, send_col, recv_row, degree, w_self, w_neigh, bias, cotangent):
    F, owned = node_feats.shape
    nz = nn // nx
    nblk = owned // TB
    Q = nblk // nf
    H = w_self.shape[0]
    FC = F // NCH
    RZ = 2 * F // nz
    cols = Q * TB
    vmem, anyw, smem = (pl.BlockSpec(memory_space=s) for s in (pltpu.VMEM, pl.ANY, pltpu.SMEM))
    V, D = pltpu.VMEM, pltpu.SemaphoreType.DMA
    scratch = [
        V((nn, CAP, TB, TB), F32),
        V((nblk, 2 * F, TB), BF),
        V((NCH, nn, CAP, FC, TB), F32),
        V((NCH, nn, CAP, FC, TB), F32),
        V((NCH, nblk, FC, TB), F32),
        V((H, cols), F32),
        V((NCH, nf, FC, cols), F32),
        V((NCH, nf, FC, cols), F32),
        V((H, H), BF), V((H, H), BF), V((H, H), BF), V((H, H), BF),
        V((NCH, H // NCH, H), BF), V((NCH, H // NCH, H), BF),
        V((NCH, H, H // NCH), BF), V((NCH, H, H // NCH), BF),
        V((H, cols), F32), V((H, cols), F32),
        V((H, cols), BF), V((H, cols), BF),
        V((cols, H), F32),
        V((NCH, nf, Q, FC, TB), F32),
        [V((nblk, FC, TB), F32) for _ in range(NCH)],
        V((nf, Q, F, TB), F32),
        V((nblk, F, TB), F32),
        V((NCH, nn, CAP, FC, TB), F32),
        V((NCH, nn, CAP, FC, TB), F32),
        V((nblk, F, TB), F32),
        V((F, owned), F32),
        V((nf, 2 * F + 8, H), F32), V((nf, 2 * F + 8, H), F32),
        V((nz, RZ + 8, H), F32), V((nz, RZ + 8, H), F32),
        V((RZ + 8, H), F32), V((nx, RZ + 8, H), F32),
        V((RZ, H), F32), V((nz, RZ, H), F32),
        V((2, nf * nz // 2, RZ, H), F32),
        V((1, H), F32),
        D((nn,)),
        D((nf,)), D((nf,)),
        D((NCH, nn)), D((NCH, nn)),
        D((NCH, nf)), D((NCH, nf)),
        D((NCH, nf)), D((NCH, nf)),
        D((nf,)), D((nf,)),
        D((NCH, nn)), D((NCH, nn)),
        D((nf,)), D((nf,)),
        D((nz,)), D((nz,)),
        D((nx,)), D((nx,)),
        D((nz,)), D((nz,)),
        D((2, nf)), D((2, nf)),
        D((5,)),
    ]
    act, gf, gs, gn, gb = pl.pallas_call(
        functools.partial(kernel, nn, nf, nx),
        out_shape=[
            jax.ShapeDtypeStruct((cols, H), F32),
            jax.ShapeDtypeStruct((F, owned), F32),
            jax.ShapeDtypeStruct((nf * nz // 2, RZ, H), F32),
            jax.ShapeDtypeStruct((nf * nz // 2, RZ, H), F32),
            jax.ShapeDtypeStruct((1, H), F32),
        ],
        in_specs=[vmem, anyw, smem, smem, vmem, vmem, vmem, vmem, vmem],
        out_specs=[anyw] * 5,
        scratch_shapes=scratch,
        compiler_params=pltpu.CompilerParams(
            collective_id=0, has_side_effects=True, vmem_limit_bytes=50 * 1024 * 1024
        ),
    )(
        node_feats, tiles, send_col, recv_row, degree.reshape(nblk, 1, TB),
        w_self, w_neigh, bias.reshape(1, H), cotangent,
    )
    return act, gf, gs.reshape(H, H), gn.reshape(H, H), gb.reshape(H)


def solution(mesh):
    return jax.shard_map(
        functools.partial(shards, mesh.shape["node"], mesh.shape["feat"], NX),
        mesh=mesh,
        in_specs=(
            P("feat", "node"),
            P("node", None, None, None),
            P("node", None),
            P("node", None),
            P("node"),
            P(),
            P(),
            P(),
            P(("node", "feat"), None),
        ),
        out_specs=(P(("node", "feat"), None), P("feat", "node"), P(), P(), P()),
        check_vma=False,
    )
```

time: 402 us -> 159 us (0.40)
  waiting for transfers between devices: 252 us -> 0 us
  Pallas kernels: 0 us -> 147 us
  matrix products: 65.2 us -> 0 us
  blocking collectives: 31.5 us -> 0 us
  starting transfers between devices: 22.1 us -> 0 us
  between operations: 13.9 us -> 0.65 us
  other arithmetic: 5.33 us -> 0 us
    pallas_call x0 -> x1, Pallas kernels: none -> 147 us  [shards(): pl.pallas_call(functools.partial(kernel, nn, nf, nx), out_shape=[jax.Shap...]
    psum x1 -> x0, waiting for transfers between devices: 136 us -> none  [shards(): lax.psum((slice_self, slice_neigh, grad_bias_part), 'node')]
    dot_general x12 -> x0, matrix products: 65.2 us -> none  [the longest x1 16.1 us: shards(): jnp.einsum('dcfj,dcij->dcfi', picked, tiles, precision=lax.Precision.HIGH...]
    all_to_all x2 -> x0, waiting for transfers between devices: 42.8 us -> none  [the longest x1 42.8 us: shards(): lax.all_to_all(partial_value, 'node', split_axis=0, concat_axis=0, tiled=...]
    all_gather x1 -> x0, waiting for transfers between devices: 37.3 us -> none  [shards(): piece = lax.all_gather(gpre, 'feat', axis=0, tiled=True)]
    reduce_scatter x1 -> x0, waiting for transfers between devices: 35.6 us -> none  [shards(): lax.psum_scatter(first + second, 'feat', scatter_dimension=0, tiled=True)]
    all_gather x2 -> x0, blocking collectives: 31.5 us -> none  [the longest x1 18.2 us: shards(): lax.all_gather(slice_self, 'feat', axis=0, tiled=True)]
    all_to_all x2 -> x0, starting transfers between devices: 21.5 us -> none  [the longest x1 12 us: shards(): lax.all_to_all(partial_value, 'node', split_axis=0, concat_axis=0, tiled=...]
  transfers between devices with their start and end apart: 5 -> 0, of which waited for: 4 -> 0; matrix products, arithmetic and copies ran while one was open for 5% -> 0% of each run, Pallas kernels for 0% -> 0%
where the time goes in v1:
time: 159 us; the launch traced here: 158 us
  Pallas kernels  147 us (92%)
  local copies, waits for them, and re-layouts  10.5 us (7%)
    pallas_call x1, Pallas kernels, shards(): pl.pallas_call(functools.partial(kernel, nn, nf, nx), out_shape=[jax.Shap...  147 us
    unnamed x19, local copies, waits for them, and re-layouts  10.5 us

profile of v1, /device:TPU:1, one launch (start us, length us, event | category | flops | bytes accessed | tf_op | source)
XLA Modules:
  0.0 158.5 jit_solution(581187833826970701)
XLA Ops:
  0.6 0.8 copy.14.scol
  1.4 0.8 copy.15.rrow
  2.2 0.0 copy-start
  2.2 1.0 copy-done
  3.2 0.0 copy-start.1
  3.2 1.0 copy-done.1
  4.2 0.0 copy-start.2
  4.2 0.9 copy-done.2
  5.2 0.0 copy-start.3
  5.2 0.9 copy-done.3
  6.1 0.0 copy-start.4
  6.1 0.7 copy-done.4
  6.9 0.0 copy-start.5
  6.9 0.7 copy-done.5
  7.5 147.4 %shard_map.128 = (f32[512,256]{1,0:T(8,128)S(1)}, f32[32,4096]{1,0:T(8,128)S(1)}, f32[32,8,256]{2,1,0:T(8,128)S(1)}, f32[32,8,256]{2,1,0:T(8,128)S(1)}, f32[1,256]{1,0:T(1,128)S(1)}) custom-call(f32[32,4096]{1,0:T(8,128)S(1)} %copy-done, f32[32,4,128,128]{3,2,1,0:T(8,128)} %tiles.1, s32[32,4]{1,0:T(8,128)S(1)} %copy.14.scol, s32[32,4]{1,0:T(8,128)S(1)} %copy.15.rrow, ...), custom_call_target="tpu_custom_call" | custom-call | tf_op jit(solution)/shard_map/pallas_call | solution.py:514
  154.9 0.8 copy.21
  155.7 0.8 copy.22
  156.5 0.7 copy.23
  157.2 0.7 copy.24
  157.9 0.6 copy.25
Async XLA Ops:
  2.2 1.0 copy-start
  3.2 1.0 copy-start.1
  4.2 0.9 copy-start.2
  5.2 0.9 copy-start.3
  6.1 0.7 copy-start.4
  6.9 0.7 copy-start.5

commit v2 on v1

v2 whole, which is shorter than its diff:
```python
import functools

import jax
import jax.numpy as jnp
from jax import lax
from jax.experimental import pallas as pl
from jax.experimental.pallas import tpu as pltpu
from jax.sharding import PartitionSpec as P

TB = 128
CAP = 4
NX = 4
NCH = 2
BF = jnp.bfloat16
F32 = jnp.float32
NN_DIMS = (((1,), (0,)), ((), ()))
NT_DIMS = (((1,), (1,)), ((), ()))
MESH = pl.DeviceIdType.MESH


def shift(t):
    return (2 * (t % 2) - 1) * ((t + 1) // 2)


def split(x):
    hi = x.astype(BF)
    return hi, (x - hi.astype(F32)).astype(BF)


def dot(a, b, dims):
    return lax.dot_general(a, b, dims, preferred_element_type=F32)


def dot3(a, b, dims):
    return dot(a[0], b[0], dims) + dot(a[0], b[1], dims) + dot(a[1], b[0], dims)


def total(ref, n):
    return sum((ref[i] for i in range(1, n)), ref[0])


def kernel(
    nn, nf, nx,
    feats_a, tiles, scol, rrow, deg_a, wself_a, wneigh_a, bias_a, cot_a,
    act_o, gf_o, gs_o, gn_o, gb_o,
    feats, deg, wself, wneigh, bias, cot,
    tv, fs, sb, rb, acc, dr, xall, nsd, nall, wsh, wsl, wsth, wstl, wnh, wnl, wnth, wntl,
    cott, pret, gh, gl, act_v, gsd, grc, gnb, ssd, srv, bsd, brv, acc2, gf_v,
    r1s, r1r, r2s, r2r, r3s, r3r, r4s, r4r, outw, gb_v, rtab,
    isem, tsem, xss, xrs, mss, mrs, fss, frs, dss, drs, nss, nrs, gss, grs, ess, ers, sss, srs, bss, brs,
    r1ss, r1rs, r2ss, r2rs, r3ss, r3rs, r4ss, r4rs, r5ss, r5rs, osem,
):
    nz = nn // nx
    F = feats.shape[0]
    nblk = feats.shape[1] // TB
    Q = nblk // nf
    H = wself.shape[0]
    FC = F // NCH
    RX = 2 * F // nx
    mf, mn = lax.axis_index("feat"), lax.axis_index("node")
    mx, mz = mn // nz, mn % nz

    def xat(dx):
        return (mx + dx + nx) % nx

    def zat(dz):
        return (mz + dz + nz) % nz

    def remote(src, dst, ss, rs, **where):
        return pltpu.make_async_remote_copy(
            src_ref=src, dst_ref=dst, send_sem=ss, recv_sem=rs, device_id=where, device_id_type=MESH)

    barrier = pltpu.get_barrier_semaphore()

    @pl.loop(1, 7 * nx)
    def _(j):
        node = xat(j // 7) * nz + zat((j % 7 + 3) % 7 - 3)
        pl.semaphore_signal(barrier, inc=1, device_id={"node": node}, device_id_type=MESH)

    pl.semaphore_signal(barrier, inc=1, device_id={"node": mx * nz + zat(4)}, device_id_type=MESH)

    @pl.loop(1, nf)
    def _(k):
        pl.semaphore_signal(barrier, inc=1, device_id={"feat": (mf + k) % nf}, device_id_type=MESH)

    loads = [
        pltpu.make_async_copy(src, dst, isem.at[i])
        for i, (src, dst) in enumerate([
            (feats_a, feats), (wself_a, wself), (wneigh_a, wneigh), (cot_a, cot), (deg_a, deg), (bias_a, bias)])
    ]
    loads[0].start()

    def owner(x, g):
        return x * nz + zat(shift(g))

    def tile_load(x, g):
        d = owner(x, g)
        return pltpu.make_async_copy(tiles.at[d], tv.at[d], tsem.at[d])

    def order(j):
        return xat(j + 1), ((j // nx) + 2) % 4 + 1

    for g in range(3):
        tile_load(mx, g).start()

    @pl.loop(0, nx)
    def _(j):
        tile_load(xat(j + 1), 7).start()

    @pl.loop(0, 4 * nx)
    def _(j):
        x, t = order(j)
        tile_load(x, t + 2).start()

    @pl.loop(0, nx - 1)
    def _(j):
        for g in range(3):
            tile_load(xat(j + 1), g).start()

    for copy in loads[1:]:
        copy.start()
    loads[0].wait()
    for b in range(nblk):
        hi, lo = split(feats[:, b * TB:(b + 1) * TB])
        fs[b, :F] = hi
        fs[b, F:] = lo
    acc[...] = jnp.zeros_like(acc)
    acc2[...] = jnp.zeros_like(acc2)

    def tile_forward(x, g):
        d = owner(x, g)
        tile_load(x, g).wait()
        for c in range(CAP):
            lhs = fs[scol[c, d]]
            th, tl = split(tv[d, c])
            o = dot(lhs, th, NT_DIMS)
            res = o[:F] + o[F:] + dot(lhs[:F], tl, NT_DIMS)
            for h in range(NCH):
                sb[h, x, 4 * g + c] = res[h * FC:(h + 1) * FC]

    for g in range(3):
        tile_forward(mx, g)
    pl.semaphore_wait(barrier, 7 * nx - 1 + 1 + nf - 1)

    def m_copy(i):
        return remote(rrow, rtab.at[i], mss.at[i], mrs.at[i], node=mx * nz + zat(2 * i - 1))

    for i in range(2):
        m_copy(i).start()

    def x_copy(to):
        cols = pl.ds(pl.multiple_of(to * (Q * TB), Q * TB), Q * TB)
        rows = pl.ds(pl.multiple_of(mf * F, F), F)
        return remote(feats.at[:, cols], xall.at[rows, :], xss.at[to], xrs.at[mf], feat=to)

    @pl.loop(1, nf)
    def _(k):
        x_copy((mf + k) % nf).start()

    own_rows = pl.ds(pl.multiple_of(mf * F, F), F)
    xall[own_rows, :] = feats[:, pl.ds(pl.multiple_of(mf * (Q * TB), Q * TB), Q * TB)]

    def place(t):
        if not isinstance(t, int):
            return pl.ds(4 * t + 8, 4)
        return pl.ds(0, 12) if t == 0 else pl.ds(4 * t + 8, 4) if t < 5 else pl.ds(18 + 2 * t, 2)

    def f_copy(h, x, t):
        at = place(t)
        return remote(sb.at[h, x, at], rb.at[h, mx, at], fss.at[h, x, t], frs.at[h, mx, t],
                      node=x * nz + zat(shift(t)))

    def b_copy(h, x, t):
        at = place(t)
        return remote(bsd.at[h, x, at], brv.at[h, mx, at], bss.at[h, x, t], brs.at[h, mx, t],
                      node=x * nz + zat(-shift(t)))

    def f_arrived(h, x, t):
        at = place(t)
        remote(sb.at[h, x, at], rb.at[h, x, at], fss.at[h, x, t], frs.at[h, x, t],
               node=x * nz + zat(-shift(t))).wait_recv()

    def b_arrived(h, x, t):
        at = place(t)
        remote(bsd.at[h, x, at], brv.at[h, x, at], bss.at[h, x, t], brs.at[h, x, t],
               node=x * nz + zat(shift(t))).wait_recv()

    @pl.loop(0, nx)
    def _(j):
        x = xat(j + 1)
        tile_forward(x, 7)
        f_copy(0, x, 5).start()
        f_copy(0, x, 6).start()

    @pl.loop(0, 4 * nx)
    def _(j):
        x, t = order(j)
        tile_forward(x, t + 2)
        f_copy(0, x, t).start()

    @pl.loop(0, nx - 1)
    def _(j):
        x = xat(j + 1)
        for g in range(3):
            tile_forward(x, g)
        f_copy(0, x, 0).start()

    for h in range(1, NCH):
        @pl.loop(0, nx)
        def _(j):
            f_copy(h, xat(j + 1), 5).start()
            f_copy(h, xat(j + 1), 6).start()

        @pl.loop(0, 4 * nx)
        def _(j):
            x, t = order(j)
            f_copy(h, x, t).start()

        @pl.loop(0, nx - 1)
        def _(j):
            f_copy(h, xat(j + 1), 0).start()

    for copy in loads[1:]:
        copy.wait()
    ws = wself[...]
    wsh[...], wsl[...] = split(ws)
    wsth[...], wstl[...] = split(ws.T)
    for h in range(NCH):
        rows = jnp.concatenate(
            [wneigh[f * F + h * FC:f * F + (h + 1) * FC, :] for f in range(nf)], axis=0)
        wnh[h], wnl[h] = split(rows)
        wnth[h], wntl[h] = split(rows.T)
    for q in range(Q):
        cott[:, q * TB:(q + 1) * TB] = cot[q * TB:(q + 1) * TB, :].T
    bias_t = jnp.broadcast_to(bias[...], (TB, H)).T

    @pl.loop(1, nf)
    def _(k):
        frm = (mf + nf - k) % nf
        rows = pl.ds(pl.multiple_of(frm * F, F), F)
        remote(xall.at[rows, :], xall.at[rows, :], xss.at[frm], xrs.at[frm], feat=frm).wait_recv()

    for q in range(Q):
        cols = slice(q * TB, (q + 1) * TB)
        pret[:, cols] = bias_t + dot3((wsth[...], wstl[...]), split(xall[:, cols]), NN_DIMS)
    for i in range(2):
        remote(rrow, rtab.at[i], mss.at[i], mrs.at[i], node=mx * nz + zat(1 - 2 * i)).wait_recv()

    def add(h, role, vals, dest):
        @pl.loop(0, nblk // 8)
        def _(k):
            for i in range(8):
                b = k * 8 + i
                a = acc[role, h, b]
                for v, r in zip(vals, dest):
                    a = a + v * jnp.where(r == b, 1.0, 0.0)
                acc[role, h, b] = a

    def add_plane(h, x, ref):
        s = x * nz + mz
        for g in range(3):
            rows = [rrow[c, s] if g == 0 else rtab[g - 1, c, s] for c in range(CAP)]
            add(h, g, [ref[h, x, 4 * g + c] for c in range(CAP)], rows)

    def d_copy(h, i):
        return remote(acc.at[1 + i, h], dr.at[h, i], dss.at[h, i], drs.at[h, i],
                      node=mx * nz + zat(1 - 2 * i))

    for h in range(NCH):
        add_plane(h, mx, sb)

        @pl.loop(0, nx)
        def _(j):
            x = xat(-1 - j)
            for i in range(2):
                f_arrived(h, x, 5 + i)
                s = x * nz + zat(-shift(5 + i))
                add(h, 1 + i, [rb[h, x, 28 + 2 * i + c] for c in range(2)],
                    [rtab[i, 2 * i + c, s] for c in range(2)])

        @pl.loop(0, 4 * nx)
        def _(j):
            t = order(j)[1]
            x = xat(-1 - j % nx)
            f_arrived(h, x, t)
            s = x * nz + zat(-shift(t))
            side = 1 - t % 2
            add(h, 1 + side, [rb[h, x, 4 * t + 8 + c] for c in range(CAP)],
                [rtab[side, c, s] for c in range(CAP)])

        @pl.loop(0, nx - 1)
        def _(j):
            x = xat(-1 - j)
            f_arrived(h, x, 0)
            add_plane(h, x, rb)

        for i in range(2):
            d_copy(h, i).start()

    def n_copy(h, to):
        return remote(nsd.at[h, to], nall.at[h, mf], nss.at[h, to], nrs.at[h, mf], feat=to)

    for h in range(NCH):
        for i in range(2):
            remote(acc.at[1 + i, h], dr.at[h, i], dss.at[h, i], drs.at[h, i],
                   node=mx * nz + zat(2 * i - 1)).wait_recv()

        @pl.loop(0, nf)
        def _(f):
            for q in range(Q):
                b = f * Q + q
                nsd[h, f, :, q * TB:(q + 1) * TB] = acc[0, h, b] + dr[h, 0, b] + dr[h, 1, b]

        @pl.loop(1, nf)
        def _(k):
            n_copy(h, (mf + k) % nf).start()

        nall[h, mf] = nsd[h, mf]

    inv = [1.0 / deg[mf * Q + q].astype(F32) for q in range(Q)]
    for h in range(NCH):
        @pl.loop(1, nf)
        def _(k):
            frm = (mf + nf - k) % nf
            remote(nsd.at[h, frm], nall.at[h, frm], nss.at[h, frm], nrs.at[h, frm], feat=frm).wait_recv()

        for q in range(Q):
            cols = slice(q * TB, (q + 1) * TB)
            nb = nall[h, :, :, cols].reshape(nf * FC, TB) * inv[q]
            nall[h, :, :, cols] = nb.reshape(nf, FC, TB)
            pre = pret[:, cols] + dot3((wnth[h], wntl[h]), split(nb), NN_DIMS)
            pret[:, cols] = pre
            if h == NCH - 1:
                sig = 1.0 / (1.0 + jnp.exp(-pre))
                act_v[cols, :] = (pre * sig).T
                g = cott[:, cols] * (sig * (1.0 + pre * (1.0 - sig)))
                gh[:, cols], gl[:, cols] = split(g)
    act_copy = pltpu.make_async_copy(act_v, act_o, osem.at[0])
    act_copy.start()

    def g_copy(h, to):
        blocks = pl.ds(pl.multiple_of(mf * Q, Q), Q)
        return remote(gsd.at[h, to], grc[h].at[blocks], gss.at[h, to], grs.at[h, mf], feat=to)

    for h in range(NCH):
        for q in range(Q):
            cols = slice(q * TB, (q + 1) * TB)
            back = dot3((wnh[h], wnl[h]), (gh[:, cols], gl[:, cols]), NN_DIMS) * inv[q]
            for f in range(nf):
                gsd[h, f, q] = back[f * FC:(f + 1) * FC]

        @pl.loop(1, nf)
        def _(k):
            g_copy(h, (mf + k) % nf).start()

        for q in range(Q):
            grc[h][mf * Q + q] = gsd[h, mf, q]

    def r1_copy(to):
        return remote(r1s.at[to], r1r.at[mf], r1ss.at[to], r1rs.at[mf], feat=to)

    part_self = dot3(split(xall[...]), (gh[...], gl[...]), NT_DIMS)
    for f in range(nf):
        r1s[f, :F] = part_self[f * F:(f + 1) * F]
    for h in range(NCH):
        part = dot3(split(nall[h].reshape(nf * FC, Q * TB)), (gh[...], gl[...]), NT_DIMS)
        for f in range(nf):
            r1s[f, F + h * FC:F + (h + 1) * FC] = part[f * FC:(f + 1) * FC]
    ones = jnp.ones((16, Q * TB), BF)
    part_bias = (dot(ones, gh[...], NT_DIMS) + dot(ones, gl[...], NT_DIMS))[:8]
    for f in range(nf):
        r1s[f, 2 * F:] = part_bias

    @pl.loop(1, nf)
    def _(k):
        r1_copy((mf + k) % nf).start()

    r1r[mf] = r1s[mf]

    def e_copy(h, i):
        return remote(grc[h], gnb[h][i], ess.at[h, i], ers.at[h, i], node=mx * nz + zat(2 * i - 1))

    for h in range(NCH):
        @pl.loop(1, nf)
        def _(k):
            frm = (mf + nf - k) % nf
            blocks = pl.ds(pl.multiple_of(frm * Q, Q), Q)
            remote(gsd.at[h, frm], grc[h].at[blocks], gss.at[h, frm], grs.at[h, frm], feat=frm).wait_recv()

        for i in range(2):
            e_copy(h, i).start()

    def s_copy(to):
        blocks = pl.ds(pl.multiple_of(mf * Q, Q), Q)
        return remote(ssd.at[to], srv.at[blocks], sss.at[to], srs.at[mf], feat=to)

    for q in range(Q):
        cols = slice(q * TB, (q + 1) * TB)
        back = dot3((wsh[...], wsl[...]), (gh[:, cols], gl[:, cols]), NN_DIMS)
        for f in range(nf):
            ssd[f, q] = back[f * F:(f + 1) * F]

    @pl.loop(1, nf)
    def _(k):
        s_copy((mf + k) % nf).start()

    for q in range(Q):
        srv[mf * Q + q] = ssd[mf, q]

    def pick(src, r):
        return src[jnp.maximum(r, 0)] * jnp.where(r >= 0, 1.0, 0.0)

    def pick_plane(h, x, ref):
        s = x * nz + mz
        for g in range(3):
            src = grc[h] if g == 0 else gnb[h][g - 1]
            for c in range(CAP):
                ref[h, x, 4 * g + c] = pick(src, rrow[c, s] if g == 0 else rtab[g - 1, c, s])

    def pick_all(h):
        for i in range(2):
            remote(grc[h], gnb[h][i], ess.at[h, i], ers.at[h, i], node=mx * nz + zat(1 - 2 * i)).wait_recv()

        @pl.loop(0, nx)
        def _(j):
            x = xat(j + 1)
            for i in range(2):
                s = x * nz + zat(-shift(5 + i))
                for c in range(2):
                    bsd[h, x, 28 + 2 * i + c] = pick(gnb[h][i], rtab[i, 2 * i + c, s])
                b_copy(h, x, 5 + i).start()

        for t in (3, 4, 1, 2):
            @pl.loop(0, nx)
            def _(j):
                x = xat(j + 1)
                s = x * nz + zat(-shift(t))
                side = 1 - t % 2
                for c in range(CAP):
                    bsd[h, x, 4 * t + 8 + c] = pick(gnb[h][side], rtab[side, c, s])
                b_copy(h, x, t).start()

        @pl.loop(0, nx - 1)
        def _(j):
            x = xat(j + 1)
            pick_plane(h, x, bsd)
            b_copy(h, x, 0).start()

        pick_plane(h, mx, brv)

    for h in range(NCH - 1):
        pick_all(h)

    @pl.loop(1, nf)
    def _(k):
        frm = (mf + nf - k) % nf
        remote(r1s.at[frm], r1r.at[frm], r1ss.at[frm], r1rs.at[frm], feat=frm).wait_recv()

    bias_sum = sum((r1r[f, 2 * F:] for f in range(1, nf)), r1r[0, 2 * F:])
    for x in range(nx):
        rows = slice(x * RX, (x + 1) * RX)
        r2s[x, :RX] = sum((r1r[f, rows] for f in range(1, nf)), r1r[0, rows])
        r2s[x, RX:] = bias_sum

    def r2_copy(x):
        return remote(r2s.at[x], r2r.at[mx], r2ss.at[x], r2rs.at[mx], node=x * nz + mz)

    @pl.loop(1, nx)
    def _(k):
        r2_copy(xat(k)).start()

    r2r[mx] = r2s[mx]

    @pl.loop(1, nx)
    def _(k):
        x = xat(-k)
        remote(r2s.at[x], r2r.at[x], r2ss.at[x], r2rs.at[x], node=x * nz + mz).wait_recv()

    r3s[...] = total(r2r, nx)

    def r3_copy(z):
        return remote(r3s, r3r.at[mz], r3ss.at[z], r3rs.at[mz], node=mx * nz + z)

    @pl.loop(1, nz)
    def _(k):
        r3_copy(zat(k)).start()

    r3r[mz] = r3s[...]
    pick_all(NCH - 1)

    def tile_backward(x, g):
        d = owner(x, g)
        outs = []
        for c in range(CAP):
            a = jnp.concatenate([brv[h, x, 4 * g + c] for h in range(NCH)], axis=0)
            ah, al = split(a)
            th, tl = split(tv[d, c])
            o = dot(jnp.concatenate([ah, al], axis=0), th, NN_DIMS)
            outs.append(o[:F] + o[F:] + dot(ah, tl, NN_DIMS))
        dest = [scol[c, d] for c in range(CAP)]

        @pl.loop(0, nblk // 8)
        def _(k):
            for i in range(8):
                b = k * 8 + i
                a = acc2[b]
                for c in range(CAP):
                    a = a + outs[c] * jnp.where(dest[c] == b, 1.0, 0.0)
                acc2[b] = a

    for g in range(3):
        tile_backward(mx, g)

    @pl.loop(1, nz)
    def _(k):
        z = zat(-k)
        remote(r3s, r3r.at[z], r3ss.at[z], r3rs.at[z], node=mx * nz + z).wait_recv()

    grads = total(r3r, nz)
    r4s[...] = grads[:RX]
    gb_v[...] = grads[RX:RX + 1]

    def r4_copy(x):
        return remote(r4s, r4r.at[mx], r4ss.at[x], r4rs.at[mx], node=x * nz + mz)

    @pl.loop(1, nx)
    def _(k):
        r4_copy(xat(k)).start()

    r4r[mx] = r4s[...]

    @pl.loop(1, nf)
    def _(k):
        to = (mf + k) % nf
        x_copy(to).wait_send()
        r1_copy(to).wait_send()
        s_copy(to).wait_send()
        for h in range(NCH):
            n_copy(h, to).wait_send()
            g_copy(h, to).wait_send()

    for h in range(NCH):
        @pl.loop(0, nx)
        def _(j):
            f_copy(h, xat(j + 1), 5).wait_send()
            f_copy(h, xat(j + 1), 6).wait_send()

        @pl.loop(0, 4 * nx)
        def _(j):
            x, t = order(j)
            f_copy(h, x, t).wait_send()

        @pl.loop(0, nx - 1)
        def _(j):
            f_copy(h, xat(j + 1), 0).wait_send()

        for i in range(2):
            d_copy(h, i).wait_send()
            e_copy(h, i).wait_send()
    for i in range(2):
        m_copy(i).wait_send()

    @pl.loop(1, nx)
    def _(k):
        r2_copy(xat(k)).wait_send()

    @pl.loop(1, nz)
    def _(k):
        r3_copy(zat(k)).wait_send()

    @pl.loop(0, nx)
    def _(j):
        x = xat(-1 - j)
        for h in range(NCH):
            b_arrived(h, x, 5)
            b_arrived(h, x, 6)
        tile_backward(x, 7)

    def r5_copy(i, to):
        part = r4r.at[pl.ds(i * (nx // 2), nx // 2)]
        rows = pl.ds(pl.multiple_of(mf * (nx // 2), nx // 2), nx // 2)
        return remote(part, outw.at[i, rows], r5ss.at[i, to], r5rs.at[i, mf], feat=to)

    def middle(start, stop):
        @pl.loop(start, stop)
        def _(j):
            t = order(j)[1]
            x = xat(-1 - j % nx)
            for h in range(NCH):
                b_arrived(h, x, t)
            tile_backward(x, t + 2)

    middle(0, 2 * nx)

    @pl.loop(1, nx)
    def _(k):
        x = xat(-k)
        remote(r4s, r4r.at[x], r4ss.at[x], r4rs.at[x], node=x * nz + mz).wait_recv()

    for i in range(2):
        @pl.loop(1, nf)
        def _(k):
            r5_copy(i, (mf + k) % nf).start()

        for x in range(nx // 2):
            outw[i, mf * (nx // 2) + x] = r4r[i * (nx // 2) + x]
    middle(2 * nx, 4 * nx)

    @pl.loop(0, nx - 1)
    def _(j):
        x = xat(-1 - j)
        for h in range(NCH):
            b_arrived(h, x, 0)
        for g in range(3):
            tile_backward(x, g)

    @pl.loop(1, nf)
    def _(k):
        frm = (mf + nf - k) % nf
        blocks = pl.ds(pl.multiple_of(frm * Q, Q), Q)
        remote(ssd.at[frm], srv.at[blocks], sss.at[frm], srs.at[frm], feat=frm).wait_recv()

    for b in range(nblk):
        gf_v[:, b * TB:(b + 1) * TB] = srv[b] + acc2[b]
    gf_copy = pltpu.make_async_copy(gf_v, gf_o, osem.at[1])
    gf_copy.start()
    for i in range(2):
        @pl.loop(1, nf)
        def _(k):
            frm = (mf + nf - k) % nf
            part = r4r.at[pl.ds(i * (nx // 2), nx // 2)]
            rows = pl.ds(pl.multiple_of(frm * (nx // 2), nx // 2), nx // 2)
            remote(part, outw.at[i, rows], r5ss.at[i, frm], r5rs.at[i, frm], feat=frm).wait_recv()
    tail = [
        pltpu.make_async_copy(outw.at[0], gs_o, osem.at[2]),
        pltpu.make_async_copy(outw.at[1], gn_o, osem.at[3]),
        pltpu.make_async_copy(gb_v, gb_o, osem.at[4]),
    ]
    for copy in tail:
        copy.start()

    @pl.loop(1, nf)
    def _(k):
        for i in range(2):
            r5_copy(i, (mf + k) % nf).wait_send()

    @pl.loop(1, nx)
    def _(k):
        r4_copy(xat(k)).wait_send()

    for h in range(NCH):
        @pl.loop(0, nx)
        def _(j):
            b_copy(h, xat(j + 1), 5).wait_send()
            b_copy(h, xat(j + 1), 6).wait_send()

        @pl.loop(0, 4 * nx)
        def _(j):
            x, t = order(j)
            b_copy(h, x, t).wait_send()

        @pl.loop(0, nx - 1)
        def _(j):
            b_copy(h, xat(j + 1), 0).wait_send()

    act_copy.wait()
    gf_copy.wait()
    for copy in tail:
        copy.wait()


def hand_over(*refs):
    n = (len(refs) - 1) // 3
    sem = refs[-1]
    takes = [pltpu.make_async_copy(refs[i], refs[2 * n + i], sem.at[0, i]) for i in range(n)]
    gives = [pltpu.make_async_copy(refs[2 * n + i], refs[n + i], sem.at[1, i]) for i in range(n)]
    for take in takes:
        take.start()
    for take, give in zip(takes, gives):
        take.wait()
        give.start()
    for give in gives:
        give.wait()


def shards(nn, nf, nx, node_feats, tiles, send_col, recv_row, degree, w_self, w_neigh, bias, cotangent):
    F, owned = node_feats.shape
    nz = nn // nx
    nblk = owned // TB
    Q = nblk // nf
    H = w_self.shape[0]
    FC = F // NCH
    RX = 2 * F // nx
    cols = Q * TB
    slots = nz * CAP
    anyw, smem = pl.BlockSpec(memory_space=pl.ANY), pl.BlockSpec(memory_space=pltpu.SMEM)
    V, D = pltpu.VMEM, pltpu.SemaphoreType.DMA
    scratch = [
        V((F, owned), F32), V((nblk, 1, TB), jnp.int32), V((H, H), F32), V((H, H), F32),
        V((1, H), F32), V((cols, H), F32),
        V((nn, CAP, TB, TB), F32),
        V((nblk, 2 * F, TB), BF),
        V((NCH, nx, slots, FC, TB), F32), V((NCH, nx, slots, FC, TB), F32),
        V((3, NCH, nblk, FC, TB), F32), V((NCH, 2, nblk, FC, TB), F32),
        V((H, cols), F32),
        V((NCH, nf, FC, cols), F32), V((NCH, nf, FC, cols), F32),
        V((H, H), BF), V((H, H), BF), V((H, H), BF), V((H, H), BF),
        V((NCH, H // NCH, H), BF), V((NCH, H // NCH, H), BF),
        V((NCH, H, H // NCH), BF), V((NCH, H, H // NCH), BF),
        V((H, cols), F32), V((H, cols), F32),
        V((H, cols), BF), V((H, cols), BF),
        V((cols, H), F32),
        V((NCH, nf, Q, FC, TB), F32),
        [V((nblk, FC, TB), F32) for _ in range(NCH)],
        [[V((nblk, FC, TB), F32) for _ in range(2)] for _ in range(NCH)],
        V((nf, Q, F, TB), F32), V((nblk, F, TB), F32),
        V((NCH, nx, slots, FC, TB), F32), V((NCH, nx, slots, FC, TB), F32),
        V((nblk, F, TB), F32), V((F, owned), F32),
        V((nf, 2 * F + 8, H), F32), V((nf, 2 * F + 8, H), F32),
        V((nx, RX + 8, H), F32), V((nx, RX + 8, H), F32),
        V((RX + 8, H), F32), V((nz, RX + 8, H), F32),
        V((RX, H), F32), V((nx, RX, H), F32),
        V((2, nf * nx // 2, RX, H), F32), V((1, H), F32),
        pltpu.SMEM((2, CAP, nn), jnp.int32),
        D((6,)), D((nn,)),
        D((nf,)), D((nf,)),
        D((2,)), D((2,)),
        D((NCH, nx, 7)), D((NCH, nx, 7)),
        D((NCH, 2)), D((NCH, 2)),
        D((NCH, nf)), D((NCH, nf)),
        D((NCH, nf)), D((NCH, nf)),
        D((NCH, 2)), D((NCH, 2)),
        D((nf,)), D((nf,)),
        D((NCH, nx, 7)), D((NCH, nx, 7)),
        D((nf,)), D((nf,)),
        D((nx,)), D((nx,)),
        D((nz,)), D((nz,)),
        D((nx,)), D((nx,)),
        D((2, nf)), D((2, nf)),
        D((5,)),
    ]
    act, gf, gs, gn, gb = pl.pallas_call(
        functools.partial(kernel, nn, nf, nx),
        out_shape=[
            jax.ShapeDtypeStruct((cols, H), F32),
            jax.ShapeDtypeStruct((F, owned), F32),
            jax.ShapeDtypeStruct((nf * nx // 2, RX, H), F32),
            jax.ShapeDtypeStruct((nf * nx // 2, RX, H), F32),
            jax.ShapeDtypeStruct((1, H), F32),
        ],
        in_specs=[anyw, anyw, smem, smem, anyw, anyw, anyw, anyw, anyw],
        out_specs=[anyw] * 5,
        scratch_shapes=scratch,
        compiler_params=pltpu.CompilerParams(
            collective_id=0, has_side_effects=True, vmem_limit_bytes=62 * 1024 * 1024
        ),
    )(
        node_feats, tiles, send_col.T, recv_row.T, degree.reshape(nblk, 1, TB),
        w_self, w_neigh, bias.reshape(1, H), cotangent,
    )
    results = [act, gf, gs.reshape(H, H), gn.reshape(H, H), gb]
    act, gf, gs, gn, gb = pl.pallas_call(
        hand_over,
        out_shape=[jax.ShapeDtypeStruct(r.shape, r.dtype) for r in results],
        in_specs=[anyw] * 5,
        out_specs=[anyw] * 5,
        scratch_shapes=[V(r.shape, r.dtype) for r in results] + [D((2, 5))],
        compiler_params=pltpu.CompilerParams(vmem_limit_bytes=62 * 1024 * 1024),
    )(*results)
    return act, gf, gs, gn, gb.reshape(H)


def solution(mesh):
    return jax.shard_map(
        functools.partial(shards, mesh.shape["node"], mesh.shape["feat"], NX),
        mesh=mesh,
        in_specs=(
            P("feat", "node"),
            P("node", None, None, None),
            P("node", None),
            P("node", None),
            P("node"),
            P(),
            P(),
            P(),
            P(("node", "feat"), None),
        ),
        out_specs=(P(("node", "feat"), None), P("feat", "node"), P(), P(), P()),
        check_vma=False,
    )
```

time: 159 us -> 123 us (0.77)
  Pallas kernels: 147 us -> 122 us
  local copies, waits for them, and re-layouts: 10.5 us -> 0 us
    pallas_call x1, Pallas kernels: 147 us -> 120 us  [shards(): pl.pallas_call(functools.partial(kernel, nn, nf, nx), out_shape=[jax.Shap...]
    unnamed x19 -> x0, local copies, waits for them, and re-layouts: 10.5 us -> none
    pallas_call x0 -> x1, Pallas kernels: none -> 2.27 us  [shards(): pl.pallas_call(hand_over, out_shape=[jax.ShapeDtypeStruct(r.shape, r.dtyp...]
where the time goes in v2:
time: 123 us
  Pallas kernels  122 us (99%)
    pallas_call x1, Pallas kernels, shards(): pl.pallas_call(functools.partial(kernel, nn, nf, nx), out_shape=[jax.Shap...  120 us

profile of v2, /device:TPU:1, one launch (start us, length us, event | category | flops | bytes accessed | tf_op | source)
XLA Modules:
  0.0 122.9 jit_solution(11497839003695915363)
XLA Ops:
  0.6 120.0 %shard_map.128 = (f32[512,256]{1,0:T(8,128)}, f32[32,4096]{1,0:T(8,128)}, f32[16,16,256]{2,1,0:T(8,128)}, f32[16,16,256]{2,1,0:T(8,128)}, f32[1,256]{1,0:T(1,128)}) custom-call(f32[32,4096]{1,0:T(8,128)} %feats_a.1, f32[32,4,128,128]{3,2,1,0:T(8,128)} %tiles.1, s32[4,32]{1,0:T(4,128)} %bitcast.10, s32[4,32]{1,0:T(4,128)} %bitcast.11, s32[32,1,128]{2,1,0:T(1,128)} %bitcast.9, ...), custom_call_target="tpu_custom_call" | custom-call | tf_op jit(solution)/shard_map/pallas_call | solution.py:742
  120.6 2.3 %shard_map.129 = (f32[512,256]{1,0:T(8,128)}, f32[32,4096]{1,0:T(8,128)}, f32[256,256]{1,0:T(8,128)}, f32[256,256]{1,0:T(8,128)}, f32[1,256]{1,0:T(1,128)}) custom-call(f32[512,256]{1,0:T(8,128)} %get-tuple-element.15.refs_0_, f32[32,4096]{1,0:T(8,128)} %get-tuple-element.16.refs_1_, f32[256,256]{1,0:T(8,128)} %bitcast.7, f32[256,256]{1,0:T(8,128)} %bitcast.8, ...), custom_call_target="tpu_custom_call" | custom-call | tf_op jit(solution)/shard_map/pallas_call | solution.py:762

commit v3 on v2

v3 whole, which is shorter than its diff:
```python
import functools

import jax
import jax.numpy as jnp
from jax import lax
from jax.experimental import pallas as pl
from jax.experimental.pallas import tpu as pltpu
from jax.sharding import PartitionSpec as P

TB = 128
CAP = 4
NX = 4
NCH = 2
BF = jnp.bfloat16
F32 = jnp.float32
NN_DIMS = (((1,), (0,)), ((), ()))
NT_DIMS = (((1,), (1,)), ((), ()))
MESH = pl.DeviceIdType.MESH


def shift(t):
    return (2 * (t % 2) - 1) * ((t + 1) // 2)


def split(x):
    hi = x.astype(BF)
    return hi, (x - hi.astype(F32)).astype(BF)


def dot(a, b, dims):
    return lax.dot_general(a, b, dims, preferred_element_type=F32)


def dot3(a, b, dims):
    return dot(a[0], b[0], dims) + dot(a[0], b[1], dims) + dot(a[1], b[0], dims)


def total(ref, n):
    return sum((ref[i] for i in range(1, n)), ref[0])


def kernel(
    nn, nf, nx,
    feats_a, tiles, scol, rrow, deg_a, wself_a, wneigh_a, bias_a, cot_a,
    act_o, gf_o, gs_o, gn_o, gb_o,
    feats, deg, wself, wneigh, bias, cot,
    tv, tb, fs, sb, rb, acc, dr, xall, nsd, nall, wsh, wsl, wsth, wstl, wnh, wnl, wnth, wntl,
    cott, pret, gh, gl, act_v, gsd, grc, gnb, ssd, srv, bsd, brv, acc2, gf_v,
    r1s, r1r, r2s, r2r, r3s, r3r, r4s, r4r, outw, gb_v, rtab,
    isem, tsem, xss, xrs, mss, mrs, fss, frs, frn, dss, drs, nss, nrs, gss, grs, ess, ers, sss, srs, bss, brs, brn,
    r1ss, r1rs, r2ss, r2rs, r3ss, r3rs, r4ss, r4rs, r5ss, r5rs, osem,
):
    nz = nn // nx
    F = feats.shape[0]
    nblk = feats.shape[1] // TB
    Q = nblk // nf
    H = wself.shape[0]
    FC = F // NCH
    RX = 2 * F // nx
    W = FC // 8
    mf, mn = lax.axis_index("feat"), lax.axis_index("node")
    mx, mz = mn // nz, mn % nz

    def xat(dx):
        return (mx + dx + nx) % nx

    def zat(dz):
        return (mz + dz + nz) % nz

    def remote(src, dst, ss, rs, **where):
        return pltpu.make_async_remote_copy(
            src_ref=src, dst_ref=dst, send_sem=ss, recv_sem=rs, device_id=where, device_id_type=MESH)

    loads = [
        pltpu.make_async_copy(src, dst, isem.at[i])
        for i, (src, dst) in enumerate([
            (feats_a, feats), (wself_a, wself), (wneigh_a, wneigh), (cot_a, cot), (deg_a, deg), (bias_a, bias)])
    ]
    loads[0].start()
    def drain(ref, sem):
        pltpu.make_async_copy(ref, ref, sem).wait()

    barrier = pltpu.get_barrier_semaphore()

    @pl.loop(1, 7 * nx)
    def _(j):
        node = xat(j // 7) * nz + zat((j % 7 + 3) % 7 - 3)
        pl.semaphore_signal(barrier, inc=1, device_id={"node": node}, device_id_type=MESH)

    pl.semaphore_signal(barrier, inc=1, device_id={"node": mx * nz + zat(4)}, device_id_type=MESH)

    @pl.loop(1, nf)
    def _(k):
        pl.semaphore_signal(barrier, inc=1, device_id={"feat": (mf + k) % nf}, device_id_type=MESH)

    def owner(x, g):
        return x * nz + zat(shift(g))

    def tile_load(x, g, sem):
        d = owner(x, g)
        pltpu.make_async_copy(tiles.at[d], tv.at[d], sem).start()

    def pair(j):
        return [2 * (j % (nx // 2)) + i for i in range(2)]

    def turn(j):
        return pair(j), ((j // (nx // 2)) + 2) % 4 + 1

    for g in range(3):
        tile_load(mx, g, tsem.at[0])

    @pl.loop(0, nx // 2)
    def _(j):
        for k in pair(j):
            tile_load(xat(k + 1), 7, tsem.at[1 + j])

    @pl.loop(0, 2 * nx)
    def _(j):
        ks, t = turn(j)
        for k in ks:
            tile_load(xat(k + 1), t + 2, tsem.at[1 + nx // 2 + j])

    @pl.loop(0, nx - 1)
    def _(k):
        for g in range(3):
            tile_load(xat(k + 1), g, tsem.at[1 + nx // 2 + 2 * nx + k])

    for copy in loads[1:]:
        copy.start()
    loads[0].wait()
    for b in range(nblk):
        hi, lo = split(feats[:, b * TB:(b + 1) * TB])
        fs[b, :F, :TB] = hi
        fs[b, :F, TB:] = hi
        fs[b, F:, :TB] = lo
        fs[b, F:, TB:] = jnp.zeros_like(lo)
    acc[...] = jnp.zeros_like(acc)
    acc2[...] = jnp.zeros_like(acc2)

    def tile_forward(x, g):
        d = owner(x, g)
        for c in range(CAP):
            halves = jnp.concatenate(split(tv[d, c]), axis=1)
            tb[d, c] = halves
            o = dot(fs[scol[c, d]], halves, NT_DIMS)
            res = o[:F] + o[F:]
            for h in range(NCH):
                sb[h, x, 4 * g + c] = res[h * FC:(h + 1) * FC]

    drain(tv.at[pl.ds(0, 3)], tsem.at[0])
    for g in range(3):
        tile_forward(mx, g)
    pl.semaphore_wait(barrier, 7 * nx - 1 + 1 + nf - 1)

    def m_copy(i):
        return remote(rrow, rtab.at[i], mss, mrs, node=mx * nz + zat(2 * i - 1))

    for i in range(2):
        m_copy(i).start()

    def x_copy(to):
        cols = pl.ds(pl.multiple_of(to * (Q * TB), Q * TB), Q * TB)
        rows = pl.ds(pl.multiple_of(mf * F, F), F)
        return remote(feats.at[:, cols], xall.at[rows, :], xss, xrs, feat=to)

    @pl.loop(1, nf)
    def _(k):
        x_copy((mf + k) % nf).start()

    own_rows = pl.ds(pl.multiple_of(mf * F, F), F)
    xall[own_rows, :] = feats[:, pl.ds(pl.multiple_of(mf * (Q * TB), Q * TB), Q * TB)]

    def place(t):
        if not isinstance(t, int):
            return pl.ds(4 * t + 8, 4)
        return pl.ds(0, 12) if t == 0 else pl.ds(4 * t + 8, 4) if t < 5 else pl.ds(18 + 2 * t, 2)

    def arrival(per_pair, single, h, k, t):
        return single.at[h, k] if isinstance(t, int) and t == 0 else per_pair.at[h, k // 2, t - 1]

    def f_copy(h, k, t):
        x, at = xat(k + 1), place(t)
        return remote(sb.at[h, x, at], rb.at[h, mx, at], fss.at[k // (nx - 1)], arrival(frs, frn, h, k, t),
                      node=x * nz + zat(shift(t)))

    def b_copy(h, k, t):
        x, at = xat(k + 1), place(t)
        return remote(bsd.at[h, x, at], brv.at[h, mx, at], bss.at[k // (nx - 1)], arrival(brs, brn, h, k, t),
                      node=x * nz + zat(-shift(t)))

    def f_arrived(h, k, t):
        count = 1 if isinstance(t, int) and t == 0 else 2
        drain(rb.at[h, pl.ds(0, count), place(t)], arrival(frs, frn, h, k, t))

    def b_arrived(h, k, t):
        count = 1 if isinstance(t, int) and t == 0 else 2
        drain(brv.at[h, pl.ds(0, count), place(t)], arrival(brs, brn, h, k, t))

    @pl.loop(0, nx // 2)
    def _(j):
        drain(tv.at[pl.ds(0, 2)], tsem.at[1 + j])
        for k in pair(j):
            tile_forward(xat(k + 1), 7)
            f_copy(0, k, 5).start()
            f_copy(0, k, 6).start()

    @pl.loop(0, 2 * nx)
    def _(j):
        ks, t = turn(j)
        drain(tv.at[pl.ds(0, 2)], tsem.at[1 + nx // 2 + j])
        for k in ks:
            tile_forward(xat(k + 1), t + 2)
            f_copy(0, k, t).start()

    @pl.loop(0, nx - 1)
    def _(k):
        drain(tv.at[pl.ds(0, 3)], tsem.at[1 + nx // 2 + 2 * nx + k])
        for g in range(3):
            tile_forward(xat(k + 1), g)
        f_copy(0, k, 0).start()

    for h in range(1, NCH):
        @pl.loop(0, nx)
        def _(k):
            f_copy(h, k, 5).start()
            f_copy(h, k, 6).start()

        @pl.loop(0, 2 * nx)
        def _(j):
            ks, t = turn(j)
            for k in ks:
                f_copy(h, k, t).start()

        @pl.loop(0, nx - 1)
        def _(k):
            f_copy(h, k, 0).start()

    for copy in loads[1:]:
        copy.wait()
    ws = wself[...]
    wsh[...], wsl[...] = split(ws)
    wsth[...], wstl[...] = split(ws.T)
    for h in range(NCH):
        rows = jnp.concatenate(
            [wneigh[f * F + h * FC:f * F + (h + 1) * FC, :] for f in range(nf)], axis=0)
        wnh[h], wnl[h] = split(rows)
        wnth[h], wntl[h] = split(rows.T)
    for q in range(Q):
        cott[:, q * TB:(q + 1) * TB] = cot[q * TB:(q + 1) * TB, :].T
    bias_t = jnp.broadcast_to(bias[...], (TB, H)).T

    if nf > 1:
        drain(xall.at[pl.ds(0, (nf - 1) * F)], xrs)
    for q in range(Q):
        cols = slice(q * TB, (q + 1) * TB)
        pret[:, cols] = bias_t + dot3((wsth[...], wstl[...]), split(xall[:, cols]), NN_DIMS)
    drain(rtab, mrs)

    def add(to, vals, dest):
        tiles_of = [v.reshape(-1, 8, TB) for v in vals]
        wanted = [jnp.full((8, TB), r, jnp.int32) for r in dest]

        @pl.loop(0, nblk // 8)
        def _(k):
            near = [w - k * 8 for w in wanted]
            sums = [to[k * 8 + i].reshape(-1, 8, TB) for i in range(8)]
            for i in range(8):
                parts = [jnp.where((r == i)[None], v, 0.0) for v, r in zip(tiles_of, near)]
                while len(parts) > 1:
                    parts = [a + b for a, b in zip(parts[::2], parts[1::2])] + parts[len(parts) // 2 * 2:]
                sums[i] = sums[i] + parts[0]
            for i in range(8):
                to[k * 8 + i] = sums[i].reshape(to.shape[1:])

    def add_plane(h, x, ref):
        s = x * nz + mz
        for g in range(3):
            rows = [rrow[c, s] if g == 0 else rtab[g - 1, c, s] for c in range(CAP)]
            add(acc.at[g, h], [ref[h, x, 4 * g + c] for c in range(CAP)], rows)

    def d_copy(h, w, i):
        return remote(acc.at[1 + i, h, :, w], dr.at[h, i, :, w], dss, drs.at[h, w], node=mx * nz + zat(1 - 2 * i))

    for h in range(NCH):
        add_plane(h, mx, sb)

        @pl.loop(0, nx // 2)
        def _(j):
            for i in range(2):
                vals, dest = [], []
                f_arrived(h, 2 * j, 5 + i)
                for k in pair(j):
                    x = xat(-1 - k)
                    s = x * nz + zat(-shift(5 + i))
                    vals += [rb[h, x, 28 + 2 * i + c] for c in range(2)]
                    dest += [rtab[i, 2 * i + c, s] for c in range(2)]
                add(acc.at[1 + i, h], vals, dest)

        @pl.loop(0, 2 * nx)
        def _(j):
            ks, t = turn(j)
            side = 1 - t % 2
            vals, dest = [], []
            f_arrived(h, ks[0], t)
            for k in ks:
                x = xat(-1 - k)
                s = x * nz + zat(-shift(t))
                vals += [rb[h, x, 4 * t + 8 + c] for c in range(CAP)]
                dest += [rtab[side, c, s] for c in range(CAP)]
            add(acc.at[1 + side, h], vals, dest)

        @pl.loop(0, nx - 1)
        def _(k):
            f_arrived(h, k, 0)
            add_plane(h, xat(-1 - k), rb)

        for w in range(W):
            for i in range(2):
                d_copy(h, w, i).start()

    def n_copy(h, w, to):
        rows = pl.ds(8 * w, 8)
        return remote(nsd.at[h, to, rows], nall.at[h, mf, rows], nss, nrs.at[h, w], feat=to)

    for h in range(NCH):
        for w in range(W):
            drain(dr.at[h, :, :, w], drs.at[h, w])

            @pl.loop(0, nf)
            def _(f):
                for q in range(Q):
                    b = f * Q + q
                    nsd[h, f, w * 8:(w + 1) * 8, q * TB:(q + 1) * TB] = acc[0, h, b, w] + dr[h, 0, b, w] + dr[h, 1, b, w]

            @pl.loop(1, nf)
            def _(k):
                n_copy(h, w, (mf + k) % nf).start()

        nall[h, mf] = nsd[h, mf]

    inv = [1.0 / deg[mf * Q + q].astype(F32) for q in range(Q)]
    for h in range(NCH):
        for w in range(W if nf > 1 else 0):
            drain(nall.at[h, pl.ds(0, nf - 1), pl.ds(8 * w, 8)], nrs.at[h, w])

        for q in range(Q):
            cols = slice(q * TB, (q + 1) * TB)
            nb = nall[h, :, :, cols].reshape(nf * FC, TB) * inv[q]
            nall[h, :, :, cols] = nb.reshape(nf, FC, TB)
            pre = pret[:, cols] + dot3((wnth[h], wntl[h]), split(nb), NN_DIMS)
            if h < NCH - 1:
                pret[:, cols] = pre
            else:
                sig = 1.0 / (1.0 + jnp.exp(-pre))
                pret[:, cols] = pre * sig
                g = cott[:, cols] * (sig * (1.0 + pre * (1.0 - sig)))
                gh[:, cols], gl[:, cols] = split(g)
    def g_copy(h, w, to):
        blocks, rows = pl.ds(pl.multiple_of(mf * Q, Q), Q), pl.ds(8 * w, 8)
        return remote(gsd.at[h, to, :, rows], grc[h].at[blocks, rows], gss, grs.at[h, w], feat=to)

    for h in range(NCH):
        for q in range(Q):
            cols = slice(q * TB, (q + 1) * TB)
            back = dot3((wnh[h], wnl[h]), (gh[:, cols], gl[:, cols]), NN_DIMS) * inv[q]
            for f in range(nf):
                gsd[h, f, q] = back[f * FC:(f + 1) * FC]

        for w in range(W):
            @pl.loop(1, nf)
            def _(k):
                g_copy(h, w, (mf + k) % nf).start()

        for q in range(Q):
            grc[h][mf * Q + q] = gsd[h, mf, q]

    def r1_copy(to):
        return remote(r1s.at[to], r1r.at[mf], r1ss, r1rs, feat=to)

    part_self = dot3(split(xall[...]), (gh[...], gl[...]), NT_DIMS)
    for f in range(nf):
        r1s[f, :F] = part_self[f * F:(f + 1) * F]
    for h in range(NCH):
        part = dot3(split(nall[h].reshape(nf * FC, Q * TB)), (gh[...], gl[...]), NT_DIMS)
        for f in range(nf):
            r1s[f, F + h * FC:F + (h + 1) * FC] = part[f * FC:(f + 1) * FC]
    ones = jnp.ones((16, Q * TB), BF)
    part_bias = (dot(ones, gh[...], NT_DIMS) + dot(ones, gl[...], NT_DIMS))[:8]
    for f in range(nf):
        r1s[f, 2 * F:] = part_bias

    @pl.loop(1, nf)
    def _(k):
        r1_copy((mf + k) % nf).start()

    r1r[mf] = r1s[mf]

    def e_copy(h, w, i):
        rows = pl.ds(8 * w, 8)
        return remote(grc[h].at[:, rows], gnb[h][i].at[:, rows], ess, ers.at[h], node=mx * nz + zat(2 * i - 1))

    for h in range(NCH):
        for w in range(W):
            if nf > 1:
                drain(grc[h].at[pl.ds(0, (nf - 1) * Q), pl.ds(8 * w, 8)], grs.at[h, w])
            for i in range(2):
                e_copy(h, w, i).start()

    for q in range(Q):
        cols = slice(q * TB, (q + 1) * TB)
        act_v[cols, :] = pret[:, cols].T
    act_copy = pltpu.make_async_copy(act_v, act_o, osem.at[0])
    act_copy.start()

    def s_copy(to):
        blocks = pl.ds(pl.multiple_of(mf * Q, Q), Q)
        return remote(ssd.at[to], srv.at[blocks], sss, srs, feat=to)

    for q in range(Q):
        cols = slice(q * TB, (q + 1) * TB)
        back = dot3((wsh[...], wsl[...]), (gh[:, cols], gl[:, cols]), NN_DIMS)
        for f in range(nf):
            ssd[f, q] = back[f * F:(f + 1) * F]

    @pl.loop(1, nf)
    def _(k):
        s_copy((mf + k) % nf).start()

    for q in range(Q):
        srv[mf * Q + q] = ssd[mf, q]

    def pick(src, r):
        return src[jnp.maximum(r, 0)] * jnp.where(r >= 0, 1.0, 0.0)

    def pick_plane(h, x, ref):
        s = x * nz + mz
        for g in range(3):
            src = grc[h] if g == 0 else gnb[h][g - 1]
            for c in range(CAP):
                ref[h, x, 4 * g + c] = pick(src, rrow[c, s] if g == 0 else rtab[g - 1, c, s])

    def pick_all(h):
        drain(acc.at[pl.ds(0, 2), h], ers.at[h])

        @pl.loop(0, nx)
        def _(j):
            x = xat(j + 1)
            for i in range(2):
                s = x * nz + zat(-shift(5 + i))
                for c in range(2):
                    bsd[h, x, 28 + 2 * i + c] = pick(gnb[h][i], rtab[i, 2 * i + c, s])
                b_copy(h, j, 5 + i).start()

        for t in (3, 4, 1, 2):
            @pl.loop(0, nx)
            def _(j):
                x = xat(j + 1)
                s = x * nz + zat(-shift(t))
                side = 1 - t % 2
                for c in range(CAP):
                    bsd[h, x, 4 * t + 8 + c] = pick(gnb[h][side], rtab[side, c, s])
                b_copy(h, j, t).start()

        @pl.loop(0, nx - 1)
        def _(j):
            x = xat(j + 1)
            pick_plane(h, x, bsd)
            b_copy(h, j, 0).start()

        pick_plane(h, mx, brv)

    HALF = NCH // 2

    if nf > 1:
        drain(r1r.at[pl.ds(0, nf - 1)], r1rs)
    bias_sum = sum((r1r[f, 2 * F:] for f in range(1, nf)), r1r[0, 2 * F:])
    for x in range(nx):
        rows = slice(x * RX, (x + 1) * RX)
        r2s[x, :RX] = sum((r1r[f, rows] for f in range(1, nf)), r1r[0, rows])
        r2s[x, RX:] = bias_sum

    def r2_copy(x):
        return remote(r2s.at[x], r2r.at[mx], r2ss, r2rs, node=x * nz + mz)

    @pl.loop(1, nx)
    def _(k):
        r2_copy(xat(k)).start()

    r2r[mx] = r2s[mx]
    for h in range(HALF):
        pick_all(h)

    drain(r2r.at[pl.ds(0, nx - 1)], r2rs)
    r3s[...] = total(r2r, nx)

    def r3_copy(z):
        return remote(r3s, r3r.at[mz], r3ss, r3rs, node=mx * nz + z)

    @pl.loop(1, nz)
    def _(k):
        r3_copy(zat(k)).start()

    r3r[mz] = r3s[...]
    for h in range(HALF, NCH):
        pick_all(h)

    others = (nf - 1) * nx // 2
    if nf > 1:
        drain(xall.at[pl.ds(0, (nf - 1) * F)], xss)
        drain(r1s.at[pl.ds(0, nf - 1)], r1ss)
        drain(nsd.at[:, pl.ds(0, nf - 1)], nss)
        drain(gsd.at[:, pl.ds(0, nf - 1)], gss)
    drain(sb.at[:, pl.ds(0, nx - 1)], fss.at[0])
    drain(sb.at[:, 0, pl.ds(0, 20)], fss.at[1])
    drain(acc.at[pl.ds(0, 2)], dss)
    drain(acc.at[pl.ds(0, 2)], ess)
    drain(rtab, mss)
    drain(r2r.at[pl.ds(0, nx - 1)], r2ss)

    def tile_backward(p, groups):
        outs, dest = [], []
        for x, g in groups:
            d = owner(x, g)
            for c in range(CAP):
                a = jnp.concatenate([brv[h, x, 4 * g + c] for h in range(p * HALF, (p + 1) * HALF)], axis=0)
                o = dot(jnp.concatenate(split(a), axis=0), tb[d, c], NN_DIMS)
                outs.append(o[:F // 2, :TB] + o[F // 2:, :TB] + o[:F // 2, TB:])
                dest.append(scol[c, d])
        add(acc2.at[p], outs, dest)

    def arrived(p, k, t):
        for h in range(p * HALF, (p + 1) * HALF):
            b_arrived(h, k, t)

    def near(p):
        @pl.loop(0, nx - 1)
        def _(k):
            arrived(p, k, 0)
            tile_backward(p, [(xat(-1 - k), g) for g in range(3)])

    def far(p):
        @pl.loop(0, nx // 2)
        def _(j):
            arrived(p, 2 * j, 5)
            arrived(p, 2 * j, 6)
            tile_backward(p, [(xat(-1 - k), 7) for k in pair(j)])

    def middle(p, start, stop):
        @pl.loop(start, stop)
        def _(j):
            ks, t = turn(j)
            arrived(p, ks[0], t)
            tile_backward(p, [(xat(-1 - k), t + 2) for k in ks])

    for p in range(2):
        tile_backward(p, [(mx, g) for g in range(3)])
    near(0)
    far(0)
    middle(0, 0, 2 * nx)

    drain(r3r.at[pl.ds(0, nz - 1)], r3rs)
    grads = total(r3r, nz)
    r4s[...] = grads[:RX]
    gb_v[...] = grads[RX:RX + 1]

    def r4_copy(x):
        return remote(r4s, r4r.at[mx], r4ss, r4rs, node=x * nz + mz)

    @pl.loop(1, nx)
    def _(k):
        r4_copy(xat(k)).start()

    r4r[mx] = r4s[...]

    drain(r3r.at[pl.ds(0, nz - 1)], r3ss)
    if nf > 1:
        drain(ssd.at[pl.ds(0, nf - 1)], sss)

    def r5_copy(i, to):
        part = r4r.at[pl.ds(i * (nx // 2), nx // 2)]
        rows = pl.ds(pl.multiple_of(mf * (nx // 2), nx // 2), nx // 2)
        return remote(part, outw.at[i, rows], r5ss, r5rs, feat=to)

    near(1)

    drain(r4r.at[pl.ds(0, nx - 1)], r4rs)
    for i in range(2):
        @pl.loop(1, nf)
        def _(k):
            r5_copy(i, (mf + k) % nf).start()

        for x in range(nx // 2):
            outw[i, mf * (nx // 2) + x] = r4r[i * (nx // 2) + x]
    far(1)
    middle(1, 0, 2 * nx)

    if nf > 1:
        drain(srv.at[pl.ds(0, (nf - 1) * Q)], srs)
    for b in range(nblk):
        gf_v[:, b * TB:(b + 1) * TB] = srv[b] + jnp.concatenate([acc2[0, b], acc2[1, b]], axis=0)
    gf_copy = pltpu.make_async_copy(gf_v, gf_o, osem.at[1])
    gf_copy.start()
    if nf > 1:
        drain(outw.at[:, pl.ds(0, others)], r5rs)
    tail = [
        pltpu.make_async_copy(outw.at[0], gs_o, osem.at[2]),
        pltpu.make_async_copy(outw.at[1], gn_o, osem.at[3]),
        pltpu.make_async_copy(gb_v, gb_o, osem.at[4]),
    ]
    for copy in tail:
        copy.start()

    if nf > 1:
        drain(outw.at[:, pl.ds(0, others)], r5ss)
    drain(r4r.at[pl.ds(0, nx - 1)], r4ss)
    drain(bsd.at[:, pl.ds(0, nx - 1)], bss.at[0])
    drain(bsd.at[:, 0, pl.ds(0, 20)], bss.at[1])
    act_copy.wait()
    gf_copy.wait()
    for copy in tail:
        copy.wait()


def hand_over(*refs):
    n = (len(refs) - 1) // 3
    sem = refs[-1]
    takes = [pltpu.make_async_copy(refs[i], refs[2 * n + i], sem.at[0, i]) for i in range(n)]
    gives = [pltpu.make_async_copy(refs[2 * n + i], refs[n + i], sem.at[1, i]) for i in range(n)]
    for take in takes:
        take.start()
    for take, give in zip(takes, gives):
        take.wait()
        give.start()
    for give in gives:
        give.wait()


def shards(nn, nf, nx, node_feats, tiles, send_col, recv_row, degree, w_self, w_neigh, bias, cotangent):
    F, owned = node_feats.shape
    nz = nn // nx
    nblk = owned // TB
    Q = nblk // nf
    H = w_self.shape[0]
    FC = F // NCH
    RX = 2 * F // nx
    cols = Q * TB
    slots = nz * CAP
    anyw, smem = pl.BlockSpec(memory_space=pl.ANY), pl.BlockSpec(memory_space=pltpu.SMEM)
    V, D = pltpu.VMEM, pltpu.SemaphoreType.DMA
    scratch = [
        V((F, owned), F32), V((nblk, 1, TB), jnp.int32), V((H, H), F32), V((H, H), F32),
        V((1, H), F32), V((cols, H), F32),
        V((nn, CAP, TB, TB), F32), V((nn, CAP, TB, 2 * TB), BF),
        V((nblk, 2 * F, 2 * TB), BF),
        V((NCH, nx, slots, FC, TB), F32), V((NCH, nx, slots, FC, TB), F32),
        V((3, NCH, nblk, FC // 8, 8, TB), F32), V((NCH, 2, nblk, FC // 8, 8, TB), F32),
        V((H, cols), F32),
        V((NCH, nf, FC, cols), F32), V((NCH, nf, FC, cols), F32),
        V((H, H), BF), V((H, H), BF), V((H, H), BF), V((H, H), BF),
        V((NCH, H // NCH, H), BF), V((NCH, H // NCH, H), BF),
        V((NCH, H, H // NCH), BF), V((NCH, H, H // NCH), BF),
        V((H, cols), F32), V((H, cols), F32),
        V((H, cols), BF), V((H, cols), BF),
        V((cols, H), F32),
        V((NCH, nf, Q, FC, TB), F32),
        [V((nblk, FC, TB), F32) for _ in range(NCH)],
        [[V((nblk, FC, TB), F32) for _ in range(2)] for _ in range(NCH)],
        V((nf, Q, F, TB), F32), V((nblk, F, TB), F32),
        V((NCH, nx, slots, FC, TB), F32), V((NCH, nx, slots, FC, TB), F32),
        V((2, nblk, F // 2, TB), F32), V((F, owned), F32),
        V((nf, 2 * F + 8, H), F32), V((nf, 2 * F + 8, H), F32),
        V((nx, RX + 8, H), F32), V((nx, RX + 8, H), F32),
        V((RX + 8, H), F32), V((nz, RX + 8, H), F32),
        V((RX, H), F32), V((nx, RX, H), F32),
        V((2, nf * nx // 2, RX, H), F32), V((1, H), F32),
        pltpu.SMEM((2, CAP, nn), jnp.int32),
        D((6,)), D((3 * nx + nx // 2,)),
        D, D, D, D,
        D((2,)), D((NCH, nx // 2, 6)), D((NCH, nx - 1)),
        D, D((NCH, FC // 8)), D, D((NCH, FC // 8)), D, D((NCH, FC // 8)),
        D, D((NCH,)), D, D,
        D((2,)), D((NCH, nx // 2, 6)), D((NCH, nx - 1)),
        *[D] * 10,
        D((5,)),
    ]
    act, gf, gs, gn, gb = pl.pallas_call(
        functools.partial(kernel, nn, nf, nx),
        out_shape=[
            jax.ShapeDtypeStruct((cols, H), F32),
            jax.ShapeDtypeStruct((F, owned), F32),
            jax.ShapeDtypeStruct((nf * nx // 2, RX, H), F32),
            jax.ShapeDtypeStruct((nf * nx // 2, RX, H), F32),
            jax.ShapeDtypeStruct((1, H), F32),
        ],
        in_specs=[anyw, anyw, smem, smem, anyw, anyw, anyw, anyw, anyw],
        out_specs=[anyw] * 5,
        scratch_shapes=scratch,
        compiler_params=pltpu.CompilerParams(
            collective_id=0, has_side_effects=True, vmem_limit_bytes=62 * 1024 * 1024
        ),
    )(
        node_feats, tiles, send_col.T, recv_row.T, degree.reshape(nblk, 1, TB),
        w_self, w_neigh, bias.reshape(1, H), cotangent,
    )
    results = [act, gf, gs.reshape(H, H), gn.reshape(H, H), gb]
    act, gf, gs, gn, gb = pl.pallas_call(
        hand_over,
        out_shape=[jax.ShapeDtypeStruct(r.shape, r.dtype) for r in results],
        in_specs=[anyw] * 5,
        out_specs=[anyw] * 5,
        scratch_shapes=[V(r.shape, r.dtype) for r in results] + [D((2, 5))],
        compiler_params=pltpu.CompilerParams(vmem_limit_bytes=62 * 1024 * 1024),
    )(*results)
    return act, gf, gs, gn, gb.reshape(H)


def solution(mesh):
    return jax.shard_map(
        functools.partial(shards, mesh.shape["node"], mesh.shape["feat"], NX),
        mesh=mesh,
        in_specs=(
            P("feat", "node"),
            P("node", None, None, None),
            P("node", None),
            P("node", None),
            P("node"),
            P(),
            P(),
            P(),
            P(("node", "feat"), None),
        ),
        out_specs=(P(("node", "feat"), None), P("feat", "node"), P(), P(), P()),
        check_vma=False,
    )
```

time: 123 us -> 111 us (0.902)
  Pallas kernels: 122 us -> 110 us
    pallas_call x1, Pallas kernels: 120 us -> 108 us  [shards(): pl.pallas_call(functools.partial(kernel, nn, nf, nx), out_shape=[jax.Shap...]
where the time goes in v3:
time: 111 us; the launch traced here: 110 us
  Pallas kernels  110 us (99%)
    pallas_call x1, Pallas kernels, shards(): pl.pallas_call(functools.partial(kernel, nn, nf, nx), out_shape=[jax.Shap...  108 us
    pallas_call x1, Pallas kernels, shards(): pl.pallas_call(hand_over, out_shape=[jax.ShapeDtypeStruct(r.shape, r.dtyp...  2.27 us

profile of v3, /device:TPU:1, one launch (start us, length us, event | category | flops | bytes accessed | tf_op | source)
XLA Modules:
  0.0 110.4 jit_solution(14707790605779002302)
XLA Ops:
  0.6 107.5 %shard_map.128 = (f32[512,256]{1,0:T(8,128)}, f32[32,4096]{1,0:T(8,128)}, f32[16,16,256]{2,1,0:T(8,128)}, f32[16,16,256]{2,1,0:T(8,128)}, f32[1,256]{1,0:T(1,128)}) custom-call(f32[32,4096]{1,0:T(8,128)} %feats_a.1, f32[32,4,128,128]{3,2,1,0:T(8,128)} %tiles.1, s32[4,32]{1,0:T(4,128)} %bitcast.10, s32[4,32]{1,0:T(4,128)} %bitcast.11, s32[32,1,128]{2,1,0:T(1,128)} %bitcast.9, ...), custom_call_target="tpu_custom_call" | custom-call | tf_op jit(solution)/shard_map/pallas_call | solution.py:686
  108.2 2.3 %shard_map.129 = (f32[512,256]{1,0:T(8,128)}, f32[32,4096]{1,0:T(8,128)}, f32[256,256]{1,0:T(8,128)}, f32[256,256]{1,0:T(8,128)}, f32[1,256]{1,0:T(1,128)}) custom-call(f32[512,256]{1,0:T(8,128)} %get-tuple-element.15.refs_0_, f32[32,4096]{1,0:T(8,128)} %get-tuple-element.16.refs_1_, f32[256,256]{1,0:T(8,128)} %bitcast.7, f32[256,256]{1,0:T(8,128)} %bitcast.8, ...), custom_call_target="tpu_custom_call" | custom-call | tf_op jit(solution)/shard_map/pallas_call | solution.py:706

commit v4 on v3

--- a/solution.py
+++ b/solution.py
@@ -41,9 +41,9 @@
 
 def kernel(
     nn, nf, nx,
-    feats_a, tiles, scol, rrow, deg_a, wself_a, wneigh_a, bias_a, cot_a,
+    feats_a, tiles, scol_a, rrow_a, deg_a, wself_a, wneigh_a, bias_a, cot_a,
     act_o, gf_o, gs_o, gn_o, gb_o,
-    feats, deg, wself, wneigh, bias, cot,
+    feats, scol, rrow, deg, wself, wneigh, bias, cot,
     tv, tb, fs, sb, rb, acc, dr, xall, nsd, nall, wsh, wsl, wsth, wstl, wnh, wnl, wnth, wntl,
     cott, pret, gh, gl, act_v, gsd, grc, gnb, ssd, srv, bsd, brv, acc2, gf_v,
     r1s, r1r, r2s, r2r, r3s, r3r, r4s, r4r, outw, gb_v, rtab,
@@ -56,7 +56,7 @@
     Q = nblk // nf
     H = wself.shape[0]
     FC = F // NCH
-    RX = 2 * F // nx
+    RZ = 2 * F // nz
     W = FC // 8
     mf, mn = lax.axis_index("feat"), lax.axis_index("node")
     mx, mz = mn // nz, mn % nz
@@ -74,9 +74,11 @@
     loads = [
         pltpu.make_async_copy(src, dst, isem.at[i])
         for i, (src, dst) in enumerate([
-            (feats_a, feats), (wself_a, wself), (wneigh_a, wneigh), (cot_a, cot), (deg_a, deg), (bias_a, bias)])
+            (feats_a, feats), (scol_a, scol), (rrow_a, rrow), (wself_a, wself), (wneigh_a, wneigh), (cot_a, cot), (deg_a, deg), (bias_a, bias)])
     ]
-    loads[0].start()
+    for copy in loads[:3]:
+        copy.start()
+
     def drain(ref, sem):
         pltpu.make_async_copy(ref, ref, sem).wait()
 
@@ -125,9 +127,10 @@
         for g in range(3):
             tile_load(xat(k + 1), g, tsem.at[1 + nx // 2 + 2 * nx + k])
 
-    for copy in loads[1:]:
+    for copy in loads[3:]:
         copy.start()
-    loads[0].wait()
+    for copy in loads[:3]:
+        copy.wait()
     for b in range(nblk):
         hi, lo = split(feats[:, b * TB:(b + 1) * TB])
         fs[b, :F, :TB] = hi
@@ -235,7 +238,7 @@
         def _(k):
             f_copy(h, k, 0).start()
 
-    for copy in loads[1:]:
+    for copy in loads[3:]:
         copy.wait()
     ws = wself[...]
     wsh[...], wsl[...] = split(ws)
@@ -439,7 +442,7 @@
             for c in range(CAP):
                 ref[h, x, 4 * g + c] = pick(src, rrow[c, s] if g == 0 else rtab[g - 1, c, s])
 
-    def pick_all(h):
+    def pick_far(h):
         drain(acc.at[pl.ds(0, 2), h], ers.at[h])
 
         @pl.loop(0, nx)
@@ -461,6 +464,7 @@
                     bsd[h, x, 4 * t + 8 + c] = pick(gnb[h][side], rtab[side, c, s])
                 b_copy(h, j, t).start()
 
+    def pick_near(h):
         @pl.loop(0, nx - 1)
         def _(j):
             x = xat(j + 1)
@@ -474,37 +478,36 @@
     if nf > 1:
         drain(r1r.at[pl.ds(0, nf - 1)], r1rs)
     bias_sum = sum((r1r[f, 2 * F:] for f in range(1, nf)), r1r[0, 2 * F:])
-    for x in range(nx):
-        rows = slice(x * RX, (x + 1) * RX)
-        r2s[x, :RX] = sum((r1r[f, rows] for f in range(1, nf)), r1r[0, rows])
-        r2s[x, RX:] = bias_sum
-
-    def r2_copy(x):
-        return remote(r2s.at[x], r2r.at[mx], r2ss, r2rs, node=x * nz + mz)
+    for z in range(nz):
+        rows = slice(z * RZ, (z + 1) * RZ)
+        r2s[z, :RZ] = sum((r1r[f, rows] for f in range(1, nf)), r1r[0, rows])
+        r2s[z, RZ:] = bias_sum
+
+    def r2_copy(z):
+        return remote(r2s.at[z], r2r.at[mz], r2ss, r2rs, node=mx * nz + z)
+
+    @pl.loop(1, nz)
+    def _(k):
+        r2_copy(zat(k)).start()
+
+    r2r[mz] = r2s[mz]
+    for h in range(HALF):
+        pick_far(h)
+    drain(r2r.at[pl.ds(0, nz - 1)], r2rs)
+    r3s[...] = total(r2r, nz)
+
+    def r3_copy(x):
+        return remote(r3s, r3r.at[mx], r3ss, r3rs, node=x * nz + mz)
 
     @pl.loop(1, nx)
     def _(k):
-        r2_copy(xat(k)).start()
-
-    r2r[mx] = r2s[mx]
+        r3_copy(xat(k)).start()
+
+    r3r[mx] = r3s[...]
     for h in range(HALF):
-        pick_all(h)
-
-    drain(r2r.at[pl.ds(0, nx - 1)], r2rs)
-    r3s[...] = total(r2r, nx)
-
-    def r3_copy(z):
-        return remote(r3s, r3r.at[mz], r3ss, r3rs, node=mx * nz + z)
-
-    @pl.loop(1, nz)
-    def _(k):
-        r3_copy(zat(k)).start()
-
-    r3r[mz] = r3s[...]
-    for h in range(HALF, NCH):
-        pick_all(h)
-
-    others = (nf - 1) * nx // 2
+        pick_near(h)
+
+    others = (nf - 1) * nz // 2
     if nf > 1:
         drain(xall.at[pl.ds(0, (nf - 1) * F)], xss)
         drain(r1s.at[pl.ds(0, nf - 1)], r1ss)
@@ -515,7 +518,7 @@
     drain(acc.at[pl.ds(0, 2)], dss)
     drain(acc.at[pl.ds(0, 2)], ess)
     drain(rtab, mss)
-    drain(r2r.at[pl.ds(0, nx - 1)], r2ss)
+    drain(r2r.at[pl.ds(0, nz - 1)], r2ss)
 
     def tile_backward(p, groups):
         outs, dest = [], []
@@ -552,45 +555,46 @@
             arrived(p, ks[0], t)
             tile_backward(p, [(xat(-1 - k), t + 2) for k in ks])
 
-    for p in range(2):
-        tile_backward(p, [(mx, g) for g in range(3)])
-    near(0)
+    tile_backward(0, [(mx, g) for g in range(3)])
+    drain(r3r.at[pl.ds(0, nx - 1)], r3rs)
+    grads = total(r3r, nx)
+    r4s[...] = grads[:RZ]
+    gb_v[...] = grads[RZ:RZ + 1]
+
+    def r4_copy(z):
+        return remote(r4s, r4r.at[mz], r4ss, r4rs, node=mx * nz + z)
+
+    @pl.loop(1, nz)
+    def _(k):
+        r4_copy(zat(k)).start()
+
+    r4r[mz] = r4s[...]
+    for h in range(HALF, NCH):
+        pick_far(h)
+        pick_near(h)
+    tile_backward(1, [(mx, g) for g in range(3)])
     far(0)
     middle(0, 0, 2 * nx)
-
-    drain(r3r.at[pl.ds(0, nz - 1)], r3rs)
-    grads = total(r3r, nz)
-    r4s[...] = grads[:RX]
-    gb_v[...] = grads[RX:RX + 1]
-
-    def r4_copy(x):
-        return remote(r4s, r4r.at[mx], r4ss, r4rs, node=x * nz + mz)
-
-    @pl.loop(1, nx)
-    def _(k):
-        r4_copy(xat(k)).start()
-
-    r4r[mx] = r4s[...]
-
-    drain(r3r.at[pl.ds(0, nz - 1)], r3ss)
+    near(0)
+
+    drain(r4r.at[pl.ds(0, nz - 1)], r4rs)
+    drain(r3r.at[pl.ds(0, nx - 1)], r3ss)
     if nf > 1:
         drain(ssd.at[pl.ds(0, nf - 1)], sss)
 
     def r5_copy(i, to):
-        part = r4r.at[pl.ds(i * (nx // 2), nx // 2)]
-        rows = pl.ds(pl.multiple_of(mf * (nx // 2), nx // 2), nx // 2)
+        part = r4r.at[pl.ds(i * (nz // 2), nz // 2)]
+        rows = pl.ds(pl.multiple_of(mf * (nz // 2), nz // 2), nz // 2)
         return remote(part, outw.at[i, rows], r5ss, r5rs, feat=to)
 
-    near(1)
-
-    drain(r4r.at[pl.ds(0, nx - 1)], r4rs)
     for i in range(2):
         @pl.loop(1, nf)
         def _(k):
             r5_copy(i, (mf + k) % nf).start()
 
-        for x in range(nx // 2):
-            outw[i, mf * (nx // 2) + x] = r4r[i * (nx // 2) + x]
+        for z in range(nz // 2):
+            outw[i, mf * (nz // 2) + z] = r4r[i * (nz // 2) + z]
+    near(1)
     far(1)
     middle(1, 0, 2 * nx)
 
@@ -612,7 +616,7 @@
 
     if nf > 1:
         drain(outw.at[:, pl.ds(0, others)], r5ss)
-    drain(r4r.at[pl.ds(0, nx - 1)], r4ss)
+    drain(r4r.at[pl.ds(0, nz - 1)], r4ss)
     drain(bsd.at[:, pl.ds(0, nx - 1)], bss.at[0])
     drain(bsd.at[:, 0, pl.ds(0, 20)], bss.at[1])
     act_copy.wait()
@@ -642,13 +646,14 @@
     Q = nblk // nf
     H = w_self.shape[0]
     FC = F // NCH
-    RX = 2 * F // nx
+    RZ = 2 * F // nz
     cols = Q * TB
     slots = nz * CAP
-    anyw, smem = pl.BlockSpec(memory_space=pl.ANY), pl.BlockSpec(memory_space=pltpu.SMEM)
+    anyw = pl.BlockSpec(memory_space=pl.ANY)
     V, D = pltpu.VMEM, pltpu.SemaphoreType.DMA
     scratch = [
-        V((F, owned), F32), V((nblk, 1, TB), jnp.int32), V((H, H), F32), V((H, H), F32),
+        V((F, owned), F32), pltpu.SMEM((CAP, nn), jnp.int32), pltpu.SMEM((CAP, nn), jnp.int32),
+        V((nblk, 1, TB), jnp.int32), V((H, H), F32), V((H, H), F32),
         V((1, H), F32), V((cols, H), F32),
         V((nn, CAP, TB, TB), F32), V((nn, CAP, TB, 2 * TB), BF),
         V((nblk, 2 * F, 2 * TB), BF),
@@ -669,12 +674,12 @@
         V((NCH, nx, slots, FC, TB), F32), V((NCH, nx, slots, FC, TB), F32),
         V((2, nblk, F // 2, TB), F32), V((F, owned), F32),
         V((nf, 2 * F + 8, H), F32), V((nf, 2 * F + 8, H), F32),
-        V((nx, RX + 8, H), F32), V((nx, RX + 8, H), F32),
-        V((RX + 8, H), F32), V((nz, RX + 8, H), F32),
-        V((RX, H), F32), V((nx, RX, H), F32),
-        V((2, nf * nx // 2, RX, H), F32), V((1, H), F32),
+        V((nz, RZ + 8, H), F32), V((nz, RZ + 8, H), F32),
+        V((RZ + 8, H), F32), V((nx, RZ + 8, H), F32),
+        V((RZ, H), F32), V((nz, RZ, H), F32),
+        V((2, nf * nz // 2, RZ, H), F32), V((1, H), F32),
         pltpu.SMEM((2, CAP, nn), jnp.int32),
-        D((6,)), D((3 * nx + nx // 2,)),
+        D((8,)), D((3 * nx + nx // 2,)),
         D, D, D, D,
         D((2,)), D((NCH, nx // 2, 6)), D((NCH, nx - 1)),
         D, D((NCH, FC // 8)), D, D((NCH, FC // 8)), D, D((NCH, FC // 8)),
@@ -688,11 +693,11 @@
         out_shape=[
             jax.ShapeDtypeStruct((cols, H), F32),
             jax.ShapeDtypeStruct((F, owned), F32),
-            jax.ShapeDtypeStruct((nf * nx // 2, RX, H), F32),
-            jax.ShapeDtypeStruct((nf * nx // 2, RX, H), F32),
+            jax.ShapeDtypeStruct((nf * nz // 2, RZ, H), F32),
+            jax.ShapeDtypeStruct((nf * nz // 2, RZ, H), F32),
             jax.ShapeDtypeStruct((1, H), F32),
         ],
-        in_specs=[anyw, anyw, smem, smem, anyw, anyw, anyw, anyw, anyw],
+        in_specs=[anyw] * 9,
         out_specs=[anyw] * 5,
         scratch_shapes=scratch,
         compiler_params=pltpu.CompilerParams(

time: 111 us -> 111 us (level); the launches traced: 110 us -> 109 us
  Pallas kernels: 110 us -> 108 us
    pallas_call x1, Pallas kernels: 108 us -> 106 us  [shards(): pl.pallas_call(functools.partial(kernel, nn, nf, nx), out_shape=[jax.Shap...]
where the time goes in v4:
time: 111 us; the launch traced here: 109 us
  Pallas kernels  108 us (97%)
    pallas_call x1, Pallas kernels, shards(): pl.pallas_call(functools.partial(kernel, nn, nf, nx), out_shape=[jax.Shap...  106 us
    pallas_call x1, Pallas kernels, shards(): pl.pallas_call(hand_over, out_shape=[jax.ShapeDtypeStruct(r.shape, r.dtyp...  2.27 us

profile of v4, /device:TPU:1, one launch (start us, length us, event | category | flops | bytes accessed | tf_op | source)
XLA Modules:
  0.0 108.9 jit_solution(14241196356805162141)
XLA Ops:
  0.6 106.0 %shard_map.128 = (f32[512,256]{1,0:T(8,128)}, f32[32,4096]{1,0:T(8,128)}, f32[32,8,256]{2,1,0:T(8,128)}, f32[32,8,256]{2,1,0:T(8,128)}, f32[1,256]{1,0:T(1,128)}) custom-call(f32[32,4096]{1,0:T(8,128)} %feats_a.1, f32[32,4,128,128]{3,2,1,0:T(8,128)} %tiles.1, s32[4,32]{1,0:T(4,128)} %bitcast.10, s32[4,32]{1,0:T(4,128)} %bitcast.11, s32[32,1,128]{2,1,0:T(1,128)} %bitcast.9, ...), custom_call_target="tpu_custom_call" | custom-call | tf_op jit(solution)/shard_map/pallas_call | solution.py:691
  106.6 2.3 %shard_map.129 = (f32[512,256]{1,0:T(8,128)}, f32[32,4096]{1,0:T(8,128)}, f32[256,256]{1,0:T(8,128)}, f32[256,256]{1,0:T(8,128)}, f32[1,256]{1,0:T(1,128)}) custom-call(f32[512,256]{1,0:T(8,128)} %get-tuple-element.15.refs_0_, f32[32,4096]{1,0:T(8,128)} %get-tuple-element.16.refs_1_, f32[256,256]{1,0:T(8,128)} %bitcast.7, f32[256,256]{1,0:T(8,128)} %bitcast.8, ...), custom_call_target="tpu_custom_call" | custom-call | tf_op jit(solution)/shard_map/pallas_call | solution.py:711

commit v5 on v4

--- a/solution.py
+++ b/solution.py
@@ -425,10 +425,6 @@
         for f in range(nf):
             ssd[f, q] = back[f * F:(f + 1) * F]
 
-    @pl.loop(1, nf)
-    def _(k):
-        s_copy((mf + k) % nf).start()
-
     for q in range(Q):
         srv[mf * Q + q] = ssd[mf, q]
 
@@ -493,6 +489,10 @@
     r2r[mz] = r2s[mz]
     for h in range(HALF):
         pick_far(h)
+    @pl.loop(1, nf)
+    def _(k):
+        s_copy((mf + k) % nf).start()
+
     drain(r2r.at[pl.ds(0, nz - 1)], r2rs)
     r3s[...] = total(r2r, nz)
 

time: 111 us -> 110 us (level)
  no operation moved by 1% of the time
where the time goes in v5:
time: 110 us; the launch traced here: 109 us
  Pallas kernels  108 us (98%)
    pallas_call x1, Pallas kernels, shards(): pl.pallas_call(functools.partial(kernel, nn, nf, nx), out_shape=[jax.Shap...  106 us
    pallas_call x1, Pallas kernels, shards(): pl.pallas_call(hand_over, out_shape=[jax.ShapeDtypeStruct(r.shape, r.dtyp...  2.27 us

profile of v5, /device:TPU:1, one launch (start us, length us, event | category | flops | bytes accessed | tf_op | source)
XLA Modules:
  0.0 108.9 jit_solution(14607174168174490257)
XLA Ops:
  0.6 106.0 %shard_map.128 = (f32[512,256]{1,0:T(8,128)}, f32[32,4096]{1,0:T(8,128)}, f32[32,8,256]{2,1,0:T(8,128)}, f32[32,8,256]{2,1,0:T(8,128)}, f32[1,256]{1,0:T(1,128)}) custom-call(f32[32,4096]{1,0:T(8,128)} %feats_a.1, f32[32,4,128,128]{3,2,1,0:T(8,128)} %tiles.1, s32[4,32]{1,0:T(4,128)} %bitcast.10, s32[4,32]{1,0:T(4,128)} %bitcast.11, s32[32,1,128]{2,1,0:T(1,128)} %bitcast.9, ...), custom_call_target="tpu_custom_call" | custom-call | tf_op jit(solution)/shard_map/pallas_call | solution.py:691
  106.6 2.3 %shard_map.129 = (f32[512,256]{1,0:T(8,128)}, f32[32,4096]{1,0:T(8,128)}, f32[256,256]{1,0:T(8,128)}, f32[256,256]{1,0:T(8,128)}, f32[1,256]{1,0:T(1,128)}) custom-call(f32[512,256]{1,0:T(8,128)} %get-tuple-element.15.refs_0_, f32[32,4096]{1,0:T(8,128)} %get-tuple-element.16.refs_1_, f32[256,256]{1,0:T(8,128)} %bitcast.7, f32[256,256]{1,0:T(8,128)} %bitcast.8, ...), custom_call_target="tpu_custom_call" | custom-call | tf_op jit(solution)/shard_map/pallas_call | solution.py:711
